TPU v7x, 32 devices: a whole 2x2x4 slice. The times are simulated.
32 devices in a mesh: seq: 16 (over z, y, x), head: 2 (over core).
Axes of the slice: x: 2, y: 2, z: 4, core: 2. Of those that a mesh axis runs over, the one named last changes fastest.
Arguments:
- queries: bfloat16 [6144, 1536], P('seq', 'head'), may hold values from -100 to 100
- keys: bfloat16 [6144, 1536], P('seq', 'head'), may hold values from -5 to 5
- values: bfloat16 [6144, 1536], P('seq', 'head'), may hold values from -6 to 6
- membership: int32 [12, 6144, 1], P('head', 'seq'), may hold values from 0 to 63, as said below
- w_out: bfloat16 [1536, 1536], P('head'), may hold values from -0.15625 to 0.15625
Outputs:
- projected: bfloat16 [6144, 1536], P('seq', 'head')
Inputs may be any that keep to these rules, and one draw needn't show every extreme that they name: `membership`: among the 384 tokens of one index of seq, in one head, no cluster holds more than 12 tokens, and some cluster holds exactly 12.
All inputs are finite; a program needn't handle non-finite values.
Results may differ from a plain program's by a relative error of at most 0.0056.
Values may be sent and summed in bfloat16 or wider, within the bound.
No kernel may reach another device: no remote copies, remote signals or barrier semaphores. Data moves between devices by JAX's collectives and lax.ppermute only.
A program may use at most 64 MiB of HBM per device.

v0:
```python
import math

import jax
import jax.numpy as jnp
from jax import lax
from jax.sharding import PartitionSpec as P

CL_DEV = 4


NEG = -1e30


def attend(block, live, own, centers, counts, head_dim):
    scale = 1.0 / math.sqrt(head_dim)
    query = block[..., :head_dim]
    key_rows = block[..., head_dim : 2 * head_dim]
    value_rows = block[..., 2 * head_dim :]
    exact = jnp.einsum("gqd,gkd->gqk", query, key_rows, preferred_element_type=jnp.float32) * scale
    exact = jnp.where(live[:, None, :] > 0, exact, NEG)
    mean_keys = centers[:, :head_dim]
    mean_values = centers[:, head_dim:]
    weights = jnp.log(jnp.maximum(counts, 1.0))
    far_scores = (
        jnp.einsum("gqd,cd->gqc", query, mean_keys, preferred_element_type=jnp.float32) * scale
    )
    far_scores = far_scores + weights[None, None, :]
    labels = jnp.arange(counts.shape[0], dtype=jnp.int32)
    valid = (counts[None, :] > 0) & (labels[None, :] != own[:, None])
    far_scores = jnp.where(valid[:, None, :], far_scores, NEG)
    top = jnp.maximum(jnp.max(exact, -1), jnp.max(far_scores, -1))
    near = jnp.exp(exact - top[..., None])
    far = jnp.exp(far_scores - top[..., None])
    total = jnp.sum(near, -1) + jnp.sum(far, -1)
    mixed = jnp.einsum(
        "gqk,gkd->gqd", near.astype(jnp.bfloat16), value_rows, preferred_element_type=jnp.float32
    )
    mixed = mixed + jnp.einsum(
        "gqc,cd->gqd", far.astype(jnp.bfloat16), mean_values, preferred_element_type=jnp.float32
    )
    return (mixed / total[..., None]).astype(jnp.bfloat16)


def per_device(queries, keys, values, membership, w_out):
    seq_count = lax.axis_size("seq")
    rank = lax.axis_index("seq")
    tok = queries.shape[0]
    heads = membership.shape[0]
    head_dim = queries.shape[1] // heads
    clusters = CL_DEV * seq_count
    cap = max(2, (2 * tok + clusters - 1) // clusters)
    member = membership[:, :, 0]
    labels = jnp.arange(clusters, dtype=jnp.int32)
    onehot = (member[:, :, None] == labels[None, None, :]).astype(jnp.bfloat16)
    order = jnp.arange(tok, dtype=jnp.int32)
    lower = (order[:, None] > order[None, :]).astype(jnp.bfloat16)
    before = jnp.einsum("ts,hsc->htc", lower, onehot, preferred_element_type=jnp.float32)
    slot = jnp.sum(before * onehot, axis=-1).astype(jnp.int32)
    place = member * cap + slot

    def split_heads(matrix):
        return matrix.reshape(tok, heads, head_dim).transpose(1, 0, 2)

    rows = jnp.concatenate([split_heads(queries), split_heads(keys), split_heads(values)], -1)
    head_index = jnp.arange(heads, dtype=jnp.int32)[:, None]
    buffer = (
        jnp.zeros((heads, clusters * cap, 3 * head_dim), jnp.bfloat16)
        .at[head_index, place]
        .set(rows)
    )
    flags = jnp.zeros((heads, clusters * cap), jnp.bfloat16).at[head_index, place].set(1.0)
    buffer = buffer.reshape(heads, clusters, cap, 3 * head_dim)
    flags = flags.reshape(heads, clusters, cap)
    received, present = (
        lax.all_to_all(buffer, "seq", split_axis=1, concat_axis=2, tiled=True),
        lax.all_to_all(flags, "seq", split_axis=1, concat_axis=2, tiled=True),
    )
    pairs = rows[:, :, head_dim:]
    sums = jnp.einsum("htc,htd->hcd", onehot, pairs, preferred_element_type=jnp.float32)
    counts = jnp.sum(onehot, axis=1, dtype=jnp.float32)
    total_sums, counts = lax.psum((sums, counts), "seq")
    centers = (total_sums / jnp.maximum(counts, 1.0)[..., None]).astype(jnp.bfloat16)
    own = rank * CL_DEV + jnp.arange(CL_DEV, dtype=jnp.int32)

    def per_head(item):
        block, live, head_centers, head_counts = item
        return attend(block, live, own, head_centers, head_counts, head_dim)

    answers = lax.map(per_head, (received, present, centers, counts))
    returned = lax.all_to_all(answers, "seq", split_axis=2, concat_axis=1, tiled=True)
    flat = returned.reshape(heads, clusters * cap, head_dim)
    picked = jnp.take_along_axis(flat, place[:, :, None], axis=1)
    attended = picked.transpose(1, 0, 2).reshape(tok, heads * head_dim)
    partial_out = jnp.dot(attended, w_out, preferred_element_type=jnp.float32)
    return lax.psum_scatter(partial_out, "head", scatter_dimension=1, tiled=True).astype(
        jnp.bfloat16
    )


def solution(mesh):
    return jax.shard_map(
        per_device,
        mesh=mesh,
        in_specs=(
            P("seq", "head"),
            P("seq", "head"),
            P("seq", "head"),
            P("head", "seq", None),
            P("head", None),
        ),
        out_specs=P("seq", "head"),
        check_vma=False,
    )
```

profile of v0, /device:TPU:9, one launch (start us, length us, event | category | flops | bytes accessed | tf_op | source)
XLA Modules:
  0.0 368.1 jit_solution(14048509122845956387)
XLA Ops:
  6.5 0.9 copy.55
  7.8 1.3 compare_and_fusion
  9.1 0.8 multiply_reduce_fusion
  9.9 0.8 and_reduce_fusion
  10.7 20.7 %scatter_custom_fusion = bf16[4608]{0:T(1024)(128)(2,1)S(1)} fusion(s32[2304]{0:T(1024)S(1)} %reshape.124, bf16[2304]{0:T(1024)(128)(2,1)S(1)} %broadcast.101, bf16[]{:T(256)} %constant.17.clone.1), kind=kCustom, calls=%fused_computation.67 | custom fusion | bytes 9218
  32.5 6.7 %all-to-all-start = ((bf16[16,2,144]{2,1,0:T(2,128)(2,1)}), bf16[16,2,144]{2,1,0:T(2,128)(2,1)S(1)}, u32[]{:S(2)}, u32[]{:S(2)}) async-start(bf16[16,2,144]{2,1,0:T(2,128)(2,1)} %reshape.144), calls=%async_computation | async-start | bytes 32768 | tf_op jit(solution)/shard_map/all_to_all | solution.py:76
  39.8 2.1 copy.28
  41.9 1.4 copy.29
  43.3 2.1 copy.26
  45.4 2.1 copy.27
  47.5 2.5 pad_maximum_fusion
  50.0 15.4 %scatter_custom_fusion.1 = bf16[4608,384]{1,0:T(8,128)(2,1)} fusion(s32[2304]{0:T(1024)} %copy-done.6, bf16[2304,384]{1,0:T(8,128)(2,1)} %bitcast.99, bf16[]{:T(256)} %constant.17.clone.1), kind=kCustom, calls=%fused_computation.40 | custom fusion | bytes 3539456
  65.4 6.7 %reshape.105 = bf16[6,64,12,384]{3,2,1,0:T(8,128)(2,1)} reshape(bf16[4608,384]{1,0:T(8,128)(2,1)} %scatter_custom_fusion.1) | data formatting | bytes 7077888 | tf_op jit(solution)/shard_map/reshape | solution.py:72
  72.2 5.0 %copy.32 = bf16[6,64,12,384]{3,2,0,1:T(8,128)(2,1)} copy(bf16[6,64,12,384]{3,2,1,0:T(8,128)(2,1)} %reshape.105) | data formatting | bytes 7077888 | tf_op jit(solution)/shard_map/reshape | solution.py:72
  77.1 6.4 %all-to-all-start.1 = ((bf16[6,64,12,384]{3,2,0,1:T(8,128)(2,1)}), bf16[6,64,12,384]{3,2,0,1:T(8,128)(2,1)}, u32[]{:S(2)}, u32[]{:S(2)}) async-start(bf16[6,64,12,384]{3,2,0,1:T(8,128)(2,1)} %copy.32), calls=%async_computation.1 | async-start | bytes 9437184 | tf_op jit(solution)/shard_map/all_to_all | solution.py:75
  83.5 1.8 fusion.26
  85.4 1.4 convert_reduce_fusion
  86.8 122.5 %psum.14 = f32[6,64]{1,0:T(8,128)} all-reduce(f32[6,64]{1,0:T(8,128)} %convert_reduce_fusion), channel_id=1, replica_groups=mesh['seq'=16,'head'=2] {'seq'}, use_global_device_ids=true, to_apply=%region_5.0 | all-reduce | flops 384 | bytes 3072 | tf_op jit(solution)/shard_map/psum | solution.py:81
  209.3 1.3 broadcast_maximum_fusion
  210.5 0.8 reshape.145
  211.3 0.9 copy.24
  212.9 1.0 all_to_all.40
  213.9 34.5 %all-reduce.2.cloned.1.call-done = f32[6,64,256]{2,1,0:T(8,128)} async-done(((f32[6,64,256]{2,1,0:T(8,128)}), f32[6,64,256]{2,1,0:T(8,128)}) %all-reduce.2.cloned.1.call-update) | async-done | bytes 393232 | tf_op jit(solution)/shard_map/psum | solution.py:81
  248.4 1.8 divide_convert_fusion
  250.2 6.5 %copy.42 = bf16[6,16,4,12,384]{4,2,3,1,0:T(4,128)(2,1)} copy(bf16[6,16,4,12,384]{4,3,0,2,1:T(8,128)(2,1)} %bitcast.12) | data formatting | bytes 7077888 | tf_op jit(solution)/shard_map/all_to_all | solution.py:75
  256.8 31.7 %while.11 = (s32[]{:T(128)}, bf16[6,4,192,128]{3,1,0,2:T(4,128)(2,1)S(1)}, bf16[6,4,192]{2,1,0:T(4,128)(2,1)S(1)}, bf16[6,4,192,384]{3,1,2,0:T(4,128)(2,1)}, f32...) while((s32[]{:T(128)}, bf16[6,4,192,128]{3,1,0,2:T(4,128)(2,1)S(1)}, ...), condition=%wide.region_11.12_spmd.clone, body=%wide.region_6.11_spmd.clone.sunk | while | flops 102383488 | bytes 7296529 | solution.py:89
  256.8 1.3 constant_dynamic-slice_fusion.3
  258.9 0.8 dynamic-slice_bitcast_fusion.2
  262.0 1.3 constant_dynamic-slice_fusion.3
  264.2 0.8 dynamic-slice_bitcast_fusion.2
  267.3 1.3 constant_dynamic-slice_fusion.3
  269.5 0.8 dynamic-slice_bitcast_fusion.2
  272.6 1.3 constant_dynamic-slice_fusion.3
  274.7 0.8 dynamic-slice_bitcast_fusion.2
  277.9 1.3 constant_dynamic-slice_fusion.3
  280.0 0.8 dynamic-slice_bitcast_fusion.2
  283.2 1.3 constant_dynamic-slice_fusion.3
  285.3 0.8 dynamic-slice_bitcast_fusion.2
  288.5 1.0 copy-done.1
  289.5 5.5 %all-to-all-start.2 = ((bf16[6,4,192,128]{3,1,0,2:T(4,128)(2,1)}), bf16[6,4,192,128]{3,1,0,2:T(4,128)(2,1)S(1)}, u32[]{:S(2)}, u32[]{:S(2)}) async-start(bf16[6,4,192,128]{3,1,0,2:T(4,128)(2,1)} %copy-done.1), calls=%async_computation.2 | async-start | bytes 2359296 | tf_op jit(solution)/shard_map/all_to_all | solution.py:90
  297.1 25.1 %all-to-all-done.2 = bf16[6,4,192,128]{3,1,0,2:T(4,128)(2,1)S(1)} async-done(((bf16[6,4,192,128]{3,1,0,2:T(4,128)(2,1)}), bf16[6,4,192,128]{3,1,0,2:T(4,128)(2,1)S(1)}, u32[]{:S(2)}, u32[]{:S(2)}) %all-to-all-start.2) | async-done | bytes 1179680 | tf_op jit(solution)/shard_map/all_to_all | solution.py:90
  322.2 1.6 copy.38
  323.8 2.3 reshape.106
  326.1 17.5 %gather_fusion = bf16[2304,128]{1,0:T(8,128)(2,1)} fusion(bf16[6,768,128]{2,1,0:T(8,128)(2,1)S(1)} %reshape.106, s32[2304]{0:T(1024)S(1)} %reshape.118), kind=kCustom, calls=%fused_computation | custom fusion | bytes 1198080 | tf_op jit(solution)/shard_map/jit(take_along_axis)/gather | solution.py:92
  343.7 1.4 copy.39
  345.1 2.5 fusion.40
  347.7 11.4 %reduce-scatter.2.cloned.1.call-done = f32[384,768]{1,0:T(8,128)} async-done(((f32[384,1536]{1,0:T(8,128)}), f32[384,768]{1,0:T(8,128)}) %reduce-scatter.2.cloned.1.call-update) | async-done | bytes 1179664 | tf_op jit(solution)/shard_map/reduce_scatter | solution.py:95
  359.1 2.1 convert_element_type.43
  (126 shorter events, 24.1 us)
Async XLA Ops:
  6.5 338.6 %copy-start = (bf16[768,1536]{1,0:T(8,128)(2,1)S(1)}, bf16[768,1536]{1,0:T(8,128)(2,1)}, u32[]{:S(2)}) copy-start(bf16[768,1536]{1,0:T(8,128)(2,1)} %param.11) | copy-start | bytes 7077892
  6.5 32.6 %copy-start.2 = (bf16[384,768]{1,0:T(8,128)(2,1)S(1)}, bf16[384,768]{1,0:T(8,128)(2,1)}, u32[]{:S(2)}) copy-start(bf16[384,768]{1,0:T(8,128)(2,1)} %param.9) | copy-start | bytes 1769476
  7.4 3.2 copy-start.5
  9.1 0.8 copy-start.3
  10.7 20.7 %copy-start.6 = (s32[2304]{0:T(1024)}, s32[2304]{0:T(1024)S(1)}, u32[]{:S(2)}) copy-start(s32[2304]{0:T(1024)S(1)} %reshape.124) | copy-start | bytes 27652
  32.5 44.7 %all-to-all-start = ((bf16[16,2,144]{2,1,0:T(2,128)(2,1)}), bf16[16,2,144]{2,1,0:T(2,128)(2,1)S(1)}, u32[]{:S(2)}, u32[]{:S(2)}) async-start(bf16[16,2,144]{2,1,0:T(2,128)(2,1)} %reshape.144), calls=%async_computation | async-start | bytes 32768 | tf_op jit(solution)/shard_map/all_to_all | solution.py:76
  77.1 173.1 %all-to-all-start.1 = ((bf16[6,64,12,384]{3,2,0,1:T(8,128)(2,1)}), bf16[6,64,12,384]{3,2,0,1:T(8,128)(2,1)}, u32[]{:S(2)}, u32[]{:S(2)}) async-start(bf16[6,64,12,384]{3,2,0,1:T(8,128)(2,1)} %copy.32), calls=%async_computation.1 | async-start | bytes 9437184 | tf_op jit(solution)/shard_map/all_to_all | solution.py:75
  83.5 165.0 %all-reduce.2.cloned.1.call-start = ((), (), s32[]{:S(2)}) async-start(), calls=%async_computation.4 | async-start | bytes 786432 | tf_op jit(solution)/shard_map/psum | solution.py:81
  288.5 1.0 copy-start.1
  289.5 5.5 %copy-start.4 = (s32[6,384,1]{1,2,0:T(1,128)S(1)}, s32[6,384,1]{1,2,0:T(1,128)}, u32[]{:S(2)}) copy-start(s32[6,384,1]{1,2,0:T(1,128)} %copy-done.3) | copy-start | bytes 27652
  289.5 32.7 %all-to-all-start.2 = ((bf16[6,4,192,128]{3,1,0,2:T(4,128)(2,1)}), bf16[6,4,192,128]{3,1,0,2:T(4,128)(2,1)S(1)}, u32[]{:S(2)}, u32[]{:S(2)}) async-start(bf16[6,4,192,128]{3,1,0,2:T(4,128)(2,1)} %copy-done.1), calls=%async_computation.2 | async-start | bytes 2359296 | tf_op jit(solution)/shard_map/all_to_all | solution.py:90
  295.0 64.1 %reduce-scatter.2.cloned.1.call-start = ((), (), s32[]{:S(2)}) async-start(), calls=%async_computation.5 | async-start | bytes 3538944 | tf_op jit(solution)/shard_map/reduce_scatter | solution.py:95
Sparse Core Ops, SparseCore 0:
  89.5 158.9 all-reduce.1
  347.8 11.2 reduce-scatter.1
where the time goes:
time: 371 us; the launch traced here: 368 us
  blocking collectives  122 us (33%)
  local copies, waits for them, and re-layouts  107 us (29%)
  waiting for transfers between devices  71 us (19%)
  other arithmetic  22.7 us (6%)
  starting transfers between devices  18.6 us (5%)
  between operations  13.6 us (4%)
  matrix products  12 us (3%)
    psum x1, blocking collectives, per_device(): total_sums, counts = lax.psum((sums, counts), 'seq')  122 us
    unnamed x25, local copies, waits for them, and re-layouts  44.8 us
    psum x1, waiting for transfers between devices, per_device(): total_sums, counts = lax.psum((sums, counts), 'seq')  34.5 us
    all_to_all x1, waiting for transfers between devices, per_device(): lax.all_to_all(answers, 'seq', split_axis=2, concat_axis=1, tiled=True)  25.1 us
    gather x2, local copies, waits for them, and re-layouts, per_device(): picked = jnp.take_along_axis(flat, place[:, :, None], axis=1)  18.9 us
    reshape x2, local copies, waits for them, and re-layouts, per_device(): buffer = buffer.reshape(heads, clusters, cap, 3 * head_dim)  11.7 us
    reduce_scatter x1, waiting for transfers between devices, per_device(): lax.psum_scatter(partial_out, 'head', scatter_dimension=1, tiled=True)  11.4 us
    dynamic_slice x12, local copies, waits for them, and re-layouts, per_device(): answers = lax.map(per_head, (received, present, centers, counts))  8.08 us
  transfers between devices with their start and end apart: 5, of which 3 were waited for; matrix products, arithmetic and copies ran while one was open for 13% of the time, Pallas kernels for 0%

commit v1 on v0

v1 whole, which is shorter than its diff:
```python
import functools
import math

import jax
import jax.numpy as jnp
from jax import lax
from jax.experimental import pallas as pl
from jax.experimental.pallas import tpu as pltpu
from jax.sharding import PartitionSpec as P

CL_DEV = 4
NEG = -1e30
EMPTY = 128.0
VMEM_LIMIT = 56 * 1024 * 1024


def iota(shape, dim):
    return lax.broadcasted_iota(jnp.int32, shape, dim)


def nt_dot(a, b):
    return lax.dot_general(a, b, (((1,), (1,)), ((), ())), preferred_element_type=jnp.float32)


def nn_dot(a, b):
    return jnp.dot(a, b, preferred_element_type=jnp.float32)


def pack_kernel(rows, cap, row_ref, col_ref, q_ref, k_ref, v_ref, send_ref, place_ref):
    tok, hd = q_ref.shape
    n_seq = send_ref.shape[0]
    slots = n_seq * rows
    member = row_ref[0]
    column = col_ref[0]
    t_first, t_second = iota((tok, tok), 0), iota((tok, tok), 1)
    same = column == member
    earlier = jnp.where(same & (t_first < t_second), 1.0, 0.0)
    slot = jnp.sum(earlier, axis=0, keepdims=True).astype(jnp.int32)
    place = (member // CL_DEV) * rows + (member % CL_DEV) * cap + slot
    later = jnp.where(same & (t_second < t_first), 1.0, 0.0)
    slot_col = jnp.sum(later, axis=1, keepdims=True).astype(jnp.int32)
    place_ref[0] = (column // CL_DEV) * rows + (column % CL_DEV) * cap + slot_col
    hot = jnp.where(iota((slots, tok), 0) == place, 1.0, 0.0).astype(jnp.bfloat16)
    ones = jnp.ones((tok, hd), jnp.bfloat16)
    packed_kv = nn_dot(hot, jnp.concatenate([k_ref[...], v_ref[...]], 1))
    packed_q = nn_dot(hot, jnp.concatenate([q_ref[...], ones], 1))
    live = packed_q[:, hd:]
    mark = jnp.where(iota((slots, hd), 1) == 0, EMPTY, 0.0)
    key = packed_kv[:, :hd] + mark * (1.0 - live)
    send_ref[:, 0, :, :hd] = packed_q[:, :hd].astype(jnp.bfloat16).reshape(n_seq, rows, hd)
    send_ref[:, 0, :, hd : 2 * hd] = key.astype(jnp.bfloat16).reshape(n_seq, rows, hd)
    send_ref[:, 0, :, 2 * hd :] = packed_kv[:, hd:].astype(jnp.bfloat16).reshape(n_seq, rows, hd)


def local_cluster(index, rows, cap):
    return lax.rem(index, rows) // cap


def live_row(key):
    hd = key.shape[1]
    pick = jnp.where(iota((16, hd), 1) == 0, 1.0, 0.0).astype(jnp.bfloat16)
    first = nt_dot(pick, key)
    return jnp.where(first < 0.5 * EMPTY, 1.0, 0.0)


def centers_kernel(rows, cap, recv_ref, out_ref, acc_ref, count_ref):
    h = pl.program_id(0)
    heads = pl.num_programs(0)
    n_seq = recv_ref.shape[0]
    slots = n_seq * rows
    hd = recv_ref.shape[3] // 3
    total_rows = out_ref.shape[1]

    @pl.when(h == 0)
    def _():
        acc_ref[...] = jnp.zeros_like(acc_ref)
        count_ref[...] = jnp.zeros_like(count_ref)

    key = recv_ref[:, 0, :, hd : 2 * hd].reshape(slots, hd)
    pairs = recv_ref[:, 0, :, hd:].reshape(slots, 2 * hd)
    live = live_row(key)
    line = iota((total_rows, slots), 0) - h * CL_DEV
    cluster = local_cluster(iota((total_rows, slots), 1), rows, cap)
    chosen = jnp.where((line == cluster) & (live[:1] > 0), 1.0, 0.0)
    acc_ref[...] += nn_dot(chosen.astype(jnp.bfloat16), pairs)
    count_ref[...] += jnp.sum(chosen, axis=1, keepdims=True)

    @pl.when(h == heads - 1)
    def _():
        count = count_ref[...]
        centers = acc_ref[...] / jnp.maximum(count, 1.0)
        r, l = iota(acc_ref.shape, 0), iota(acc_ref.shape, 1)
        diagonal = jnp.sum(jnp.where(r == l, count, 0.0), axis=0, keepdims=True)
        block = jnp.where(r == heads * CL_DEV, diagonal, centers).astype(jnp.bfloat16)
        for j in range(n_seq):
            out_ref[j] = block


def attend_kernel(rows, cap, step, rank_ref, all_ref, recv_ref, out_ref, cent_ref, bias_ref, dead_ref):
    h = pl.program_id(0)
    heads = pl.num_programs(0)
    n_seq = recv_ref.shape[0]
    slots = n_seq * rows
    hd = recv_ref.shape[3] // 3
    clusters = n_seq * CL_DEV
    block = all_ref.shape[1]
    far = cent_ref.shape[1]
    root = math.sqrt(hd)

    @pl.when(h == 0)
    def _():
        everything = all_ref[...].reshape(n_seq * block, 2 * hd)
        r = iota((far, n_seq * block), 1)
        c = iota((far, n_seq * block), 0)
        inside = c < clusters
        last = (c // CL_DEV) * block + heads * CL_DEV
        tall = jnp.where((r == last) & inside, 1.0, 0.0).astype(jnp.bfloat16)
        counts = nn_dot(tall, everything)
        lane, line = iota((far, 2 * hd), 1), iota((far, 2 * hd), 0)
        ones = jnp.ones((16, 2 * hd), jnp.bfloat16)
        for i in range(heads_of(cent_ref)):
            base = (c // CL_DEV) * block + i * CL_DEV + lax.rem(c, CL_DEV)
            hot = jnp.where((r == base) & inside, 1.0, 0.0).astype(jnp.bfloat16)
            cent_ref[i] = nn_dot(hot, everything).astype(jnp.bfloat16)
            mine = jnp.where(lane == i * CL_DEV + lax.rem(line, CL_DEV), counts, 0.0)
            row = nt_dot(ones, mine.astype(jnp.bfloat16))[:8]
            bias_ref[i] = jnp.log(jnp.maximum(row, 1.0)) * root
            dead_ref[i] = jnp.broadcast_to(jnp.sum(mine, axis=1, keepdims=True), (far, hd))

    rank = rank_ref[0]
    key = recv_ref[:, 0, :, hd : 2 * hd].reshape(slots, hd)
    value = recv_ref[:, 0, :, 2 * hd :].reshape(slots, hd)
    query = recv_ref[:, 0, :, :hd].reshape(slots, hd)
    lane = iota((slots, hd), 1)
    cluster = local_cluster(iota((slots, hd), 0), rows, cap)
    query_side = jnp.where(lane == cluster, 1.0, 0.0).astype(jnp.bfloat16)
    empty = key[:, :1].astype(jnp.float32) > 0.5 * EMPTY
    key_side = jnp.where((lane == cluster) & jnp.logical_not(empty), 0.0, NEG).astype(jnp.bfloat16)
    far_lane, far_line = iota((far, hd), 1), iota((far, hd), 0)
    own = far_lane + rank * CL_DEV == far_line
    far_side = jnp.where((dead_ref[h] > 0) & jnp.logical_not(own), 0.0, NEG).astype(jnp.bfloat16)
    near_keys = jnp.concatenate([key, key_side], 1)
    centers = cent_ref[h]
    far_keys = jnp.concatenate([centers[:, :hd], far_side], 1)
    near_values = jnp.concatenate([value, jnp.ones((slots, hd), jnp.bfloat16)], 1)
    far_values = jnp.concatenate([centers[:, hd:], jnp.ones((far, hd), jnp.bfloat16)], 1)
    queries = jnp.concatenate([query, query_side], 1)
    scale = math.log2(math.e) / root
    for start in range(0, slots, step):
        q = queries[start : start + step]
        near = nt_dot(q, near_keys)
        distant = nt_dot(q, far_keys) + bias_ref[h][:1]
        top = jnp.maximum(jnp.max(near, 1, keepdims=True), jnp.max(distant, 1, keepdims=True))
        near = jnp.exp2((near - top) * scale).astype(jnp.bfloat16)
        distant = jnp.exp2((distant - top) * scale).astype(jnp.bfloat16)
        mixed = nn_dot(near, near_values) + nn_dot(distant, far_values)
        answer = (mixed[:, :hd] / mixed[:, hd:]).astype(jnp.bfloat16)
        first = start // rows
        out_ref[first : first + step // rows, 0] = answer.reshape(step // rows, rows, hd)


def heads_of(ref):
    return ref.shape[0]


def unpack_kernel(place_ref, back_ref, out_ref):
    n_seq, _, rows, hd = back_ref.shape
    tok = out_ref.shape[0]
    slots = n_seq * rows
    hot = jnp.where(iota((tok, slots), 1) == place_ref[0], 1.0, 0.0).astype(jnp.bfloat16)
    out_ref[...] = nn_dot(hot, back_ref[:, 0].reshape(slots, hd)).astype(jnp.bfloat16)


def per_device(queries, keys, values, membership, w_out):
    n_seq = lax.axis_size("seq")
    groups = lax.axis_size("head")
    rank = lax.axis_index("seq")
    group = lax.axis_index("head")
    tok = queries.shape[0]
    heads = membership.shape[0]
    hd = queries.shape[1] // heads
    width = w_out.shape[1] // groups
    clusters = CL_DEV * n_seq
    cap = max(2, (2 * tok + clusters - 1) // clusters)
    rows = (CL_DEV * cap + 15) // 16 * 16
    slots = n_seq * rows
    params = pltpu.CompilerParams(
        dimension_semantics=("arbitrary",), vmem_limit_bytes=VMEM_LIMIT
    )
    exchange = functools.partial(
        lax.all_to_all, axis_name="seq", split_axis=0, concat_axis=0, tiled=True
    )
    swap = [(i, (i + 1) % groups) for i in range(groups)]

    mine = lax.dynamic_slice_in_dim(w_out, group * width, width, 1)
    other = lax.dynamic_slice_in_dim(w_out, (1 - group) * width, width, 1)
    other = lax.ppermute(other, "head", swap)

    matrix = pl.BlockSpec((tok, hd), lambda h: (0, h))
    line = pl.BlockSpec((1, 1, tok), lambda h: (h, 0, 0))
    column = pl.BlockSpec((1, tok, 1), lambda h: (h, 0, 0))

    def slot_block(depth):
        return pl.BlockSpec((n_seq, 1, rows, depth), lambda h: (0, h, 0, 0))

    send, place = pl.pallas_call(
        functools.partial(pack_kernel, rows, cap),
        grid=(heads,),
        in_specs=[line, column, matrix, matrix, matrix],
        out_specs=[slot_block(3 * hd), column],
        out_shape=[
            jax.ShapeDtypeStruct((n_seq, heads, rows, 3 * hd), jnp.bfloat16),
            jax.ShapeDtypeStruct((heads, tok, 1), jnp.int32),
        ],
        compiler_params=params,
        name="pack",
    )(membership.reshape(heads, 1, tok), membership, queries, keys, values)
    received = exchange(send)

    center_rows = (heads * CL_DEV + 1 + 15) // 16 * 16
    centers = pl.pallas_call(
        functools.partial(centers_kernel, rows, cap),
        grid=(heads,),
        in_specs=[slot_block(3 * hd)],
        out_specs=pl.BlockSpec((n_seq, center_rows, 2 * hd), lambda h: (0, 0, 0)),
        out_shape=jax.ShapeDtypeStruct((n_seq, center_rows, 2 * hd), jnp.bfloat16),
        scratch_shapes=[
            pltpu.VMEM((center_rows, 2 * hd), jnp.float32),
            pltpu.VMEM((center_rows, 1), jnp.float32),
        ],
        compiler_params=params,
        name="centers",
    )(received)
    all_centers = exchange(centers)

    far = (clusters + 127) // 128 * 128
    step = rows
    while step * 2 <= 384 and slots % (step * 2) == 0:
        step *= 2
    answers = pl.pallas_call(
        functools.partial(attend_kernel, rows, cap, step),
        grid=(heads,),
        in_specs=[
            pl.BlockSpec(memory_space=pltpu.SMEM),
            pl.BlockSpec((n_seq, center_rows, 2 * hd), lambda h: (0, 0, 0)),
            slot_block(3 * hd),
        ],
        out_specs=slot_block(hd),
        out_shape=jax.ShapeDtypeStruct((n_seq, heads, rows, hd), jnp.bfloat16),
        scratch_shapes=[
            pltpu.VMEM((heads, far, 2 * hd), jnp.bfloat16),
            pltpu.VMEM((heads, 8, far), jnp.float32),
            pltpu.VMEM((heads, far, hd), jnp.float32),
        ],
        compiler_params=params,
        name="attend",
    )(rank.reshape(1), all_centers, received)
    returned = exchange(answers)

    attended = pl.pallas_call(
        unpack_kernel,
        grid=(heads,),
        in_specs=[column, slot_block(hd)],
        out_specs=matrix,
        out_shape=jax.ShapeDtypeStruct((tok, heads * hd), jnp.bfloat16),
        compiler_params=params,
        name="unpack",
    )(place, returned)
    partner = lax.ppermute(attended, "head", swap)
    result = nn_dot(attended, mine) + nn_dot(partner, other)
    return result.astype(jnp.bfloat16)


def solution(mesh):
    return jax.shard_map(
        per_device,
        mesh=mesh,
        in_specs=(
            P("seq", "head"),
            P("seq", "head"),
            P("seq", "head"),
            P("head", "seq", None),
            P("head", None),
        ),
        out_specs=P("seq", "head"),
        check_vma=False,
    )
```

time: 371 us -> 175 us (0.47)
  local copies, waits for them, and re-layouts: 107 us -> 5.14 us
  waiting for transfers between devices: 71 us -> 30.7 us
  blocking collectives: 122 us -> 85.2 us
  Pallas kernels: 0 us -> 34.2 us
  other arithmetic: 22.7 us -> 0 us
  between operations: 13.6 us -> 0.03 us
  matrix products: 12 us -> 4.4 us
    psum x1 -> x0, blocking collectives: 122 us -> none  [per_device(): total_sums, counts = lax.psum((sums, counts), 'seq')]
    all_to_all x0 -> x1, blocking collectives: none -> 85.2 us  [per_device(): received = exchange(send)]
    unnamed x25 -> x7, local copies, waits for them, and re-layouts: 44.8 us -> 4.03 us
    psum x1 -> x0, waiting for transfers between devices: 34.5 us -> none  [per_device(): total_sums, counts = lax.psum((sums, counts), 'seq')]
    pallas_call x0 -> x4, Pallas kernels: none -> 34.2 us  [the longest x1 14.8 us: per_device(): pl.pallas_call(functools.partial(attend_kernel, rows, cap, step), grid=(h...]
    gather x2 -> x0, local copies, waits for them, and re-layouts: 18.9 us -> none  [per_device(): picked = jnp.take_along_axis(flat, place[:, :, None], axis=1)]
    reshape x8 -> x0, local copies, waits for them, and re-layouts: 18 us -> none  [the longest x2 11.7 us: per_device(): buffer = buffer.reshape(heads, clusters, cap, 3 * head_dim)]
    reduce_scatter x1 -> x0, waiting for transfers between devices: 11.4 us -> none  [per_device(): lax.psum_scatter(partial_out, 'head', scatter_dimension=1, tiled=True)]
  transfers between devices with their start and end apart: 5 -> 4, of which waited for: 3 -> 3; matrix products, arithmetic and copies ran while one was open for 13% -> 2% of each run, Pallas kernels for 0% -> 3%
where the time goes in v1:
time: 175 us
  blocking collectives  85.2 us (49%)
  Pallas kernels  34.2 us (20%)
  waiting for transfers between devices  30.7 us (18%)
  starting transfers between devices  15.1 us (9%)
  local copies, waits for them, and re-layouts  5.14 us (3%)
  matrix products  4.4 us (3%)
    all_to_all x1, blocking collectives, per_device(): received = exchange(send)  85.2 us
    all_to_all x1, waiting for transfers between devices, per_device(): returned = exchange(answers)  23.9 us
    pallas_call x1, Pallas kernels, per_device(): pl.pallas_call(functools.partial(attend_kernel, rows, cap, step), grid=(h...  14.8 us
    pallas_call x1, Pallas kernels, per_device(): pl.pallas_call(functools.partial(pack_kernel, rows, cap), grid=(heads,),...  8.21 us
    all_to_all x1, waiting for transfers between devices, per_device(): all_centers = exchange(centers)  6.69 us
    all_to_all x1, starting transfers between devices, per_device(): returned = exchange(answers)  5.87 us
    pallas_call x1, Pallas kernels, per_device(): pl.pallas_call(unpack_kernel, grid=(heads,), in_specs=[column, slot_block...  5.67 us
    pallas_call x1, Pallas kernels, per_device(): pl.pallas_call(functools.partial(centers_kernel, rows, cap), grid=(heads,...  5.46 us
  transfers between devices with their start and end apart: 4, of which 3 were waited for; matrix products, arithmetic and copies ran while one was open for 2% of the time, Pallas kernels for 3%

profile of v1, /device:TPU:9, one launch (start us, length us, event | category | flops | bytes accessed | tf_op | source)
XLA Modules:
  0.0 174.7 jit_solution(10574094842669890433)
XLA Ops:
  0.0 0.0 copy-start
  0.0 2.3 %copy.6.col_ref = s32[6,384,1]{2,1,0:T(8,128)} copy(s32[6,384,1]{1,2,0:T(1,128)} %param.8) | data formatting | bytes 18432 | tf_op args[3]
  2.3 8.2 %pack.1 = (bf16[16,6,48,384]{3,2,1,0:T(8,128)(2,1)}, s32[6,384,1]{2,1,0:T(8,128)}) custom-call(s32[6,1,384]{2,1,0:T(1,128)} %bitcast.5, s32[6,384,1]{2,1,0:T(8,128)} %copy.6.col_ref, bf16[384,768]{1,0:T(8,128)(2,1)} %q_ref.1, bf16[384,768]{1,0:T(8,128)(2,1)} %k_ref.1, bf16[384,768]{1,0:T(8,128)(2,1)} %v_ref.1), custom_call_target="tpu_custom_call" | custom-call | tf_op jit(solution)/shard_map/pack/pallas_call | solution.py:206
  10.5 85.2 %all_to_all.15.recv_ref = bf16[16,6,48,384]{3,2,1,0:T(8,128)(2,1)} all-to-all(bf16[16,6,48,384]{3,2,1,0:T(8,128)(2,1)} %get-tuple-element.8), channel_id=1, replica_groups=mesh['seq'=16,'head'=2] {'seq'}, dimensions={0} | all-to-all | bytes 7077888 | tf_op jit(solution)/shard_map/all_to_all | solution.py:218
  95.7 5.5 %centers.1 = bf16[16,32,256]{2,1,0:T(8,128)(2,1)} custom-call(bf16[16,6,48,384]{3,2,1,0:T(8,128)(2,1)} %all_to_all.15.recv_ref), custom_call_target="tpu_custom_call" | custom-call | tf_op jit(solution)/shard_map/centers/pallas_call | solution.py:221
  101.1 4.5 %all-to-all-start.1 = ((bf16[16,32,256]{2,1,0:T(8,128)(2,1)}), bf16[16,32,256]{2,1,0:T(8,128)(2,1)S(1)}, u32[]{:S(2)}, u32[]{:S(2)}) async-start(bf16[16,32,256]{2,1,0:T(8,128)(2,1)} %centers.1), calls=%async_computation.1 | async-start | bytes 524288 | tf_op jit(solution)/shard_map/all_to_all | solution.py:234
  105.6 6.7 %all-to-all-done.1.all_ref = bf16[16,32,256]{2,1,0:T(8,128)(2,1)S(1)} async-done(((bf16[16,32,256]{2,1,0:T(8,128)(2,1)}), bf16[16,32,256]{2,1,0:T(8,128)(2,1)S(1)}, u32[]{:S(2)}, u32[]{:S(2)}) %all-to-all-start.1) | async-done | bytes 262176 | tf_op jit(solution)/shard_map/all_to_all | solution.py:234
  112.3 0.0 copy-start.2
  112.3 0.7 copy-done.2
  113.0 14.8 %attend.1 = bf16[16,6,48,128]{3,2,1,0:T(8,128)(2,1)} custom-call(s32[1]{0:T(128)} %bitcast.1.rank_ref, bf16[16,32,256]{2,1,0:T(8,128)(2,1)} %copy-done.2, bf16[16,6,48,384]{3,2,1,0:T(8,128)(2,1)} %all_to_all.15.recv_ref), custom_call_target="tpu_custom_call" | custom-call | tf_op jit(solution)/shard_map/attend/pallas_call | solution.py:240
  127.8 5.9 %all-to-all-start.2 = ((bf16[16,6,48,128]{3,2,1,0:T(8,128)(2,1)}), bf16[16,6,48,128]{3,2,1,0:T(8,128)(2,1)S(1)}, u32[]{:S(2)}, u32[]{:S(2)}) async-start(bf16[16,6,48,128]{3,2,1,0:T(8,128)(2,1)} %attend.1), calls=%async_computation.2 | async-start | bytes 2359296 | tf_op jit(solution)/shard_map/all_to_all | solution.py:258
  133.7 0.0 copy-done
  133.7 1.1 constant_dynamic-slice_fusion
  134.8 2.2 %collective-permute-start.1 = (bf16[768,768]{1,0:T(8,128)(2,1)}, bf16[768,768]{1,0:T(8,128)(2,1)}, u32[]{:S(2)}, u32[]{:S(2)}) collective-permute-start(bf16[768,768]{1,0:T(8,128)(2,1)} %constant_dynamic-slice_fusion), channel_id=1, source_target_pairs={{0,1},{1,0},{2,3},{3,2},{4,5},{5,4},{6,7},{7,6},{8,9},{9,8},{10,11... | collective-permute-start | bytes 3538952 | tf_op jit(solution)/shard_map/ppermute | solution.py:197
  136.9 23.9 %all-to-all-done.2.back_ref = bf16[16,6,48,128]{3,2,1,0:T(8,128)(2,1)S(1)} async-done(((bf16[16,6,48,128]{3,2,1,0:T(8,128)(2,1)}), bf16[16,6,48,128]{3,2,1,0:T(8,128)(2,1)S(1)}, u32[]{:S(2)}, u32[]{:S(2)}) %all-to-all-start.2) | async-done | bytes 1179680 | tf_op jit(solution)/shard_map/all_to_all | solution.py:258
  160.9 0.0 copy-start.1
  160.9 1.0 copy-done.1
  161.9 5.7 %unpack.1 = bf16[384,768]{1,0:T(8,128)(2,1)} custom-call(s32[6,384,1]{2,1,0:T(8,128)} %get-tuple-element.7.place_ref, bf16[16,6,48,128]{3,2,1,0:T(8,128)(2,1)} %copy-done.1), custom_call_target="tpu_custom_call" | custom-call | tf_op jit(solution)/shard_map/unpack/pallas_call | solution.py:260
  167.6 2.6 %collective-permute-start = (bf16[384,768]{1,0:T(8,128)(2,1)}, bf16[384,768]{1,0:T(8,128)(2,1)S(1)}, u32[]{:S(2)}, u32[]{:S(2)}) collective-permute-start(bf16[384,768]{1,0:T(8,128)(2,1)} %unpack.1), channel_id=1, source_target_pairs={{0,1},{1,0},{2,3},{3,2},{4,5},{5,4},{6,7},{7,6},{8,9},{9,8},{10,11... | collective-permute-start | bytes 1769480 | tf_op jit(solution)/shard_map/ppermute | solution.py:269
  170.1 1.7 fusion.1
  171.8 0.0 collective-permute-done.1
  171.8 0.1 collective-permute-done
  171.9 2.7 %fusion = bf16[384,768]{1,0:T(8,128)(2,1)} fusion(f32[384,768]{1,0:T(8,128)S(1)} %fusion.1, bf16[384,768]{1,0:T(8,128)(2,1)S(1)} %collective-permute-done, bf16[768,768]{1,0:T(8,128)(2,1)} %collective-permute-done.1), kind=kOutput, calls=%fused_computation.1 | convolution fusion | flops 453574656 | bytes 3538944 | tf_op jit(solution)/shard_map/dot_general | solution.py:26
Async XLA Ops:
  0.0 133.7 %copy-start = (bf16[768,1536]{1,0:T(8,128)(2,1)S(1)}, bf16[768,1536]{1,0:T(8,128)(2,1)}, u32[]{:S(2)}) copy-start(bf16[768,1536]{1,0:T(8,128)(2,1)} %param.9) | copy-start | bytes 7077892
  101.1 11.2 %all-to-all-start.1 = ((bf16[16,32,256]{2,1,0:T(8,128)(2,1)}), bf16[16,32,256]{2,1,0:T(8,128)(2,1)S(1)}, u32[]{:S(2)}, u32[]{:S(2)}) async-start(bf16[16,32,256]{2,1,0:T(8,128)(2,1)} %centers.1), calls=%async_computation.1 | async-start | bytes 524288 | tf_op jit(solution)/shard_map/all_to_all | solution.py:234
  112.3 0.7 copy-start.2
  127.8 33.0 %all-to-all-start.2 = ((bf16[16,6,48,128]{3,2,1,0:T(8,128)(2,1)}), bf16[16,6,48,128]{3,2,1,0:T(8,128)(2,1)S(1)}, u32[]{:S(2)}, u32[]{:S(2)}) async-start(bf16[16,6,48,128]{3,2,1,0:T(8,128)(2,1)} %attend.1), calls=%async_computation.2 | async-start | bytes 2359296 | tf_op jit(solution)/shard_map/all_to_all | solution.py:258
  134.8 37.0 %collective-permute-start.1 = (bf16[768,768]{1,0:T(8,128)(2,1)}, bf16[768,768]{1,0:T(8,128)(2,1)}, u32[]{:S(2)}, u32[]{:S(2)}) collective-permute-start(bf16[768,768]{1,0:T(8,128)(2,1)} %constant_dynamic-slice_fusion), channel_id=1, source_target_pairs={{0,1},{1,0},{2,3},{3,2},{4,5},{5,4},{6,7},{7,6},{8,9},{9,8},{10,11... | collective-permute-start | bytes 3538952 | tf_op jit(solution)/shard_map/ppermute | solution.py:197
  160.9 1.0 copy-start.1
  167.6 4.4 %collective-permute-start = (bf16[384,768]{1,0:T(8,128)(2,1)}, bf16[384,768]{1,0:T(8,128)(2,1)S(1)}, u32[]{:S(2)}, u32[]{:S(2)}) collective-permute-start(bf16[384,768]{1,0:T(8,128)(2,1)} %unpack.1), channel_id=1, source_target_pairs={{0,1},{1,0},{2,3},{3,2},{4,5},{5,4},{6,7},{7,6},{8,9},{9,8},{10,11... | collective-permute-start | bytes 1769480 | tf_op jit(solution)/shard_map/ppermute | solution.py:269

commit v2 on v0

v2 whole, which is shorter than its diff:
```python
import functools
import math

import jax
import jax.numpy as jnp
from jax import lax
from jax.experimental import pallas as pl
from jax.experimental.pallas import tpu as pltpu
from jax.sharding import PartitionSpec as P

CL_DEV = 4
NEG = -1e30
EMPTY = 128.0
BF16 = jnp.bfloat16
F32 = jnp.float32


def iota(shape, dim):
    return lax.broadcasted_iota(jnp.int32, shape, dim)


def nt_dot(a, b):
    return lax.dot_general(a, b, (((1,), (1,)), ((), ())), preferred_element_type=F32)


def nn_dot(a, b):
    return jnp.dot(a, b, preferred_element_type=F32)


def one_zero(mask, kind=BF16):
    return jnp.where(mask, 1.0, 0.0).astype(kind)


def pack_kv_kernel(rows, cap, member_ref, k_ref, v_ref, send_ref, place_ref, lower_ref):
    tok = k_ref.shape[0]
    n_seq, per_step = send_ref.shape[:2]
    hd = k_ref.shape[1] // per_step
    slots = n_seq * rows
    clusters = n_seq * CL_DEV

    @pl.when(pl.program_id(0) == 0)
    def _():
        lower_ref[...] = one_zero(iota((tok, tok), 0) < iota((tok, tok), 1))

    for i in range(per_step):
        member = member_ref[i]
        same = iota((clusters, tok), 0) == member
        before = nn_dot(one_zero(same), lower_ref[...])
        slot = jnp.sum(jnp.where(same, before, 0.0), axis=0, keepdims=True).astype(jnp.int32)
        place = (member // CL_DEV) * rows + (member % CL_DEV) * cap + slot
        place_ref[i] = place
        hot = one_zero(iota((slots, tok), 0) == place, F32)
        live = jnp.sum(hot, axis=1, keepdims=True)
        span = slice(i * hd, (i + 1) * hd)
        pair = jnp.concatenate([k_ref[:, span], v_ref[:, span]], 1)
        packed = nn_dot(hot.astype(BF16), pair)
        mark = jnp.where(iota((slots, 2 * hd), 1) == 0, EMPTY * (1.0 - live), 0.0)
        send_ref[:, i] = (packed + mark).astype(BF16).reshape(n_seq, rows, 2 * hd)


def pack_q_kernel(rows, place_ref, q_ref, send_ref, column_ref):
    tok = q_ref.shape[0]
    n_seq = send_ref.shape[0]
    per_step = send_ref.shape[1] // rows
    hd = q_ref.shape[1] // per_step
    slots = n_seq * rows
    h = pl.program_id(0) * per_step

    @pl.when(h == 0)
    def _():
        column_ref[...] = jnp.zeros_like(column_ref)

    for i in range(per_step):
        place = place_ref[i]
        hot = one_zero(iota((slots, tok), 0) == place)
        packed = nn_dot(hot, q_ref[:, i * hd : (i + 1) * hd])
        send_ref[:, i * rows : (i + 1) * rows] = packed.astype(BF16).reshape(n_seq, rows, hd)
        turned = jnp.broadcast_to(place.astype(F32), (128, tok)).T.astype(jnp.int32)
        column_ref[...] += jnp.where(iota((tok, 128), 1) == h + i, turned, 0)


def regroup_kernel(rows, cap, recv_ref, key_ref, value_ref, perm_ref):
    h = pl.program_id(0)
    n_seq = recv_ref.shape[0]
    slots = n_seq * rows
    near = n_seq * cap
    hd = recv_ref.shape[3] // 2

    @pl.when(h == 0)
    def _():
        line = iota((near, 1), 0)
        source = line // cap
        origin = source * rows + (line - source * cap)
        for e in range(CL_DEV):
            perm_ref[e] = one_zero(iota((near, slots), 1) == origin + e * cap)

    pairs = recv_ref[:, 0].reshape(slots, 2 * hd)
    lane = iota((near, hd), 1)
    for e in range(CL_DEV):
        grouped = nn_dot(perm_ref[e], pairs)
        live = grouped[:, :1] < 0.5 * EMPTY
        kept = jnp.where(live, grouped, 0.0).astype(BF16)
        key_ref[0, e, :, :hd] = kept[:, :hd]
        key_ref[0, e, :, hd:] = jnp.where((lane == 0) & jnp.logical_not(live), NEG, 0.0).astype(BF16)
        value_ref[0, e, :, :hd] = kept[:, hd:]
        value_ref[0, e, :, hd:] = jnp.ones((near, hd), BF16)


def centers_kernel(cap, heads, recv_ref, buffer_ref, send_ref, acc_ref, count_ref, block_ref, sem):
    del buffer_ref
    n_seq, per_step, rows, _ = recv_ref.shape
    extra, hd = acc_ref.shape
    owned = heads * CL_DEV
    step = pl.program_id(0)

    @pl.when(step == 0)
    def _():
        acc_ref[...] = jnp.zeros_like(acc_ref)
        count_ref[...] = jnp.zeros_like(count_ref)

    line = iota((extra, 1), 0)
    row = iota((rows, 1), 0)
    for i in range(per_step):
        key = recv_ref[:, i, :, :hd].astype(F32)
        value = recv_ref[:, i, :, hd:].astype(F32)
        live = key[:, :, :1] < 0.5 * EMPTY
        key = jnp.sum(jnp.where(live, key, 0.0), axis=0)
        value = jnp.sum(value, axis=0)
        number = jnp.sum(jnp.where(live, 1.0, 0.0), axis=0)
        for e in range(CL_DEV):
            inside = (row >= e * cap) & (row < (e + 1) * cap)
            at = (step * per_step + i) * CL_DEV + e
            key_sum = jnp.sum(jnp.where(inside, key, 0.0), axis=0, keepdims=True)
            value_sum = jnp.sum(jnp.where(inside, value, 0.0), axis=0, keepdims=True)
            count = jnp.sum(jnp.where(inside, number, 0.0), axis=0, keepdims=True)
            here, there = line == at, line == at + owned
            acc_ref[...] += jnp.where(here, key_sum, jnp.where(there, value_sum, 0.0))
            count_ref[...] += jnp.where(here | there, count, 0.0)

    @pl.when(step == pl.num_programs(0) - 1)
    def _():
        count = count_ref[...]
        centers = acc_ref[...] / jnp.maximum(count, 1.0)
        r, l = iota((extra, hd), 0), iota((extra, hd), 1)
        diagonal = jnp.sum(jnp.where(r == l, count, 0.0), axis=0, keepdims=True)
        block = jnp.where(r == 2 * owned, diagonal, centers).astype(BF16)
        for j in range(n_seq):
            block_ref[j] = block
        copy = pltpu.make_async_copy(block_ref, send_ref.at[:, pl.ds(heads * rows, extra)], sem)
        copy.start()
        copy.wait()


def prepare_far(rank, all_centers, heads, key_ref, value_ref):
    _, far, _ = value_ref.shape
    n_seq, block, hd = all_centers.shape
    owned = heads * CL_DEV
    root = math.sqrt(hd)
    everything = all_centers.reshape(n_seq * block, hd)
    r, c = iota((far, n_seq * block), 1), iota((far, n_seq * block), 0)
    base = (c // CL_DEV) * block
    counts = nn_dot(one_zero(r == base + 2 * owned), everything)
    lane, line = iota((far, hd), 1), iota((far, hd), 0)
    cluster = line % CL_DEV
    own = (line // CL_DEV == rank) & (lane == cluster + 3)
    base = r - base - c % CL_DEV
    for h in range(heads):
        key = nn_dot(one_zero(base == h * CL_DEV), everything)
        value = nn_dot(one_zero(base == h * CL_DEV + owned), everything)
        count = jnp.sum(
            jnp.where(lane - cluster == h * CL_DEV, counts, 0.0), axis=1, keepdims=True
        )
        bias = jnp.where(count > 0, jnp.log(jnp.maximum(count, 1.0)) * root, NEG)
        high = bias.astype(BF16).astype(F32)
        middle = (bias - high).astype(BF16).astype(F32)
        low = bias - high - middle
        side = jnp.where(lane == 0, high, jnp.where(lane == 1, middle, jnp.where(lane == 2, low, 0.0)))
        side = jnp.where(own, NEG, side)
        key_ref[h, :, :hd] = key.astype(BF16)
        key_ref[h, :, hd:] = side.astype(BF16)
        value_ref[h, :, :hd] = value.astype(BF16)
        value_ref[h, :, hd:] = jnp.ones((far, hd), BF16)


def attend_kernel(rows, cap, rank_ref, recv_ref, near_key_ref, near_value_ref, out_ref, far_key_ref, far_value_ref):
    step = pl.program_id(0)
    n_seq, per_step = out_ref.shape[:2]
    hd = recv_ref.shape[2]
    heads = far_key_ref.shape[0]

    @pl.when(step == 0)
    def _():
        prepare_far(rank_ref[0], recv_ref[:, heads * rows :], heads, far_key_ref, far_value_ref)

    group = n_seq * 16
    scale = math.log2(math.e) / math.sqrt(hd)
    lane = iota((group, hd), 1)
    row = iota((n_seq, 16, 1), 1).reshape(group, 1)
    for i in range(per_step):
        h = step * per_step + i
        far_key, far_value = far_key_ref[h], far_value_ref[h]
        keys = [jnp.concatenate([near_key_ref[i, e], far_key], 0) for e in range(CL_DEV)]
        values = [jnp.concatenate([near_value_ref[i, e], far_value], 0) for e in range(CL_DEV)]
        for tile in range(rows // 16):
            place = row + tile * 16
            clusters = [
                e for e in range(CL_DEV) if e * cap < tile * 16 + 16 and (e + 1) * cap > tile * 16
            ]
            side = jnp.where(lane < 3, 1.0, 0.0)
            for e in clusters:
                inside = (place >= e * cap) & (place < (e + 1) * cap)
                side = jnp.where((lane == 3 + e) & inside, 1.0, side)
            start = pl.multiple_of(h * rows + tile * 16, 16)
            query = recv_ref[:, pl.ds(start, 16)].reshape(group, hd)
            query = jnp.concatenate([query, side.astype(BF16)], 1)
            score = None
            for e in clusters:
                mine = nt_dot(query, keys[e])
                score = mine if score is None else jnp.where(place >= e * cap, mine, score)
            top = jnp.max(score, 1, keepdims=True)
            weight = jnp.exp2((score - top) * scale).astype(BF16)
            mixed = None
            for e in clusters:
                mine = nn_dot(weight, values[e])
                mixed = mine if mixed is None else jnp.where(place >= e * cap, mine, mixed)
            answer = (mixed[:, :hd] / mixed[:, hd:]).astype(BF16)
            out_ref[:, i, tile * 16 : tile * 16 + 16] = answer.reshape(n_seq, 16, hd)


def unpack_kernel(column_ref, back_ref, out_ref):
    n_seq, per_step, rows, hd = back_ref.shape
    tok = out_ref.shape[0]
    slots = n_seq * rows
    h = pl.program_id(0) * per_step
    column = column_ref[...]
    for i in range(per_step):
        place = jnp.sum(
            jnp.where(iota((tok, 128), 1) == h + i, column, 0), axis=1, keepdims=True
        )
        hot = one_zero(iota((tok, slots), 1) == place)
        answer = nn_dot(hot, back_ref[:, i].reshape(slots, hd))
        out_ref[:, i * hd : (i + 1) * hd] = answer.astype(BF16)


def per_device(queries, keys, values, membership, w_out):
    n_seq = lax.axis_size("seq")
    groups = lax.axis_size("head")
    rank = lax.axis_index("seq")
    group = lax.axis_index("head")
    tok = queries.shape[0]
    heads = membership.shape[0]
    hd = queries.shape[1] // heads
    width = w_out.shape[1] // groups
    clusters = CL_DEV * n_seq
    cap = max(2, (2 * tok + clusters - 1) // clusters)
    rows = (CL_DEV * cap + 15) // 16 * 16
    near = n_seq * cap
    per_step = 2
    params = pltpu.CompilerParams(
        dimension_semantics=("arbitrary",),
        vmem_limit_bytes=60 * 1024 * 1024,
    )
    exchange = functools.partial(
        lax.all_to_all, axis_name="seq", split_axis=0, concat_axis=0, tiled=True
    )
    swap = [(i, (i + 1) % groups) for i in range(groups)]

    mine = lax.dynamic_slice_in_dim(w_out, group * width, width, 1)
    other = lax.dynamic_slice_in_dim(w_out, (1 - group) * width, width, 1)
    other = lax.ppermute(other, "head", swap)

    matrix = pl.BlockSpec((tok, per_step * hd), lambda h: (0, h))
    line = pl.BlockSpec((per_step, 1, tok), lambda h: (h, 0, 0))
    column = pl.BlockSpec((tok, 128), lambda h: (0, 0))

    def slot_block(depth, count):
        return pl.BlockSpec((n_seq, count, rows, depth), lambda h: (0, h, 0, 0))

    def slot_array(depth):
        return jax.ShapeDtypeStruct((n_seq, heads, rows, depth), BF16)

    send_kv, place = pl.pallas_call(
        functools.partial(pack_kv_kernel, rows, cap),
        grid=(heads // per_step,),
        in_specs=[line, matrix, matrix],
        out_specs=[slot_block(2 * hd, per_step), line],
        out_shape=[slot_array(2 * hd), jax.ShapeDtypeStruct((heads, 1, tok), jnp.int32)],
        scratch_shapes=[pltpu.VMEM((tok, tok), BF16)],
        compiler_params=params,
        name="pack_kv",
    )(membership.reshape(heads, 1, tok), keys, values)
    received_kv = exchange(send_kv)

    extra = (2 * heads * CL_DEV + 1 + 15) // 16 * 16
    all_rows = heads * rows + extra
    q_array = jax.ShapeDtypeStruct((n_seq, all_rows, hd), BF16)
    send_q, columns = pl.pallas_call(
        functools.partial(pack_q_kernel, rows),
        grid=(heads // per_step,),
        in_specs=[line, matrix],
        out_specs=[pl.BlockSpec((n_seq, per_step * rows, hd), lambda h: (0, h, 0)), column],
        out_shape=[q_array, jax.ShapeDtypeStruct((tok, 128), jnp.int32)],
        compiler_params=params,
        name="pack_q",
    )(place, queries)

    anywhere = pl.BlockSpec(memory_space=pl.ANY)
    send_q = pl.pallas_call(
        functools.partial(centers_kernel, cap, heads),
        grid=(heads // per_step,),
        in_specs=[slot_block(2 * hd, per_step), anywhere],
        out_specs=anywhere,
        out_shape=q_array,
        scratch_shapes=[
            pltpu.VMEM((extra, hd), F32),
            pltpu.VMEM((extra, 1), F32),
            pltpu.VMEM((n_seq, extra, hd), BF16),
            pltpu.SemaphoreType.DMA,
        ],
        input_output_aliases={1: 0},
        compiler_params=params,
        name="centers",
    )(received_kv, send_q)
    received_q = exchange(send_q)

    def near_block(count):
        return pl.BlockSpec((count, CL_DEV, near, 2 * hd), lambda h: (h, 0, 0, 0))

    near_array = jax.ShapeDtypeStruct((heads, CL_DEV, near, 2 * hd), BF16)
    near_keys, near_values = pl.pallas_call(
        functools.partial(regroup_kernel, rows, cap),
        grid=(heads,),
        in_specs=[slot_block(2 * hd, 1)],
        out_specs=[near_block(1), near_block(1)],
        out_shape=[near_array, near_array],
        scratch_shapes=[pltpu.VMEM((CL_DEV, near, n_seq * rows), BF16)],
        compiler_params=params,
        name="regroup",
    )(received_kv)

    answers = pl.pallas_call(
        functools.partial(attend_kernel, rows, cap),
        grid=(heads // per_step,),
        in_specs=[
            pl.BlockSpec(memory_space=pltpu.SMEM),
            pl.BlockSpec((n_seq, all_rows, hd), lambda h: (0, 0, 0)),
            near_block(per_step),
            near_block(per_step),
        ],
        out_specs=slot_block(hd, per_step),
        out_shape=slot_array(hd),
        scratch_shapes=[
            pltpu.VMEM((heads, clusters, 2 * hd), BF16),
            pltpu.VMEM((heads, clusters, 2 * hd), BF16),
        ],
        compiler_params=params,
        name="attend",
    )(rank.reshape(1), received_q, near_keys, near_values)
    returned = exchange(answers)

    attended = pl.pallas_call(
        unpack_kernel,
        grid=(heads // per_step,),
        in_specs=[column, slot_block(hd, per_step)],
        out_specs=matrix,
        out_shape=jax.ShapeDtypeStruct((tok, heads * hd), BF16),
        compiler_params=params,
        name="unpack",
    )(columns, returned)
    partner = lax.ppermute(attended, "head", swap)
    result = nn_dot(attended, mine) + nn_dot(partner, other)
    return result.astype(BF16)


def solution(mesh):
    return jax.shard_map(
        per_device,
        mesh=mesh,
        in_specs=(
            P("seq", "head"),
            P("seq", "head"),
            P("seq", "head"),
            P("head", "seq", None),
            P("head", None),
        ),
        out_specs=P("seq", "head"),
        check_vma=False,
    )
```

time: 371 us -> 162 us (0.44)
  blocking collectives: 122 us -> 0 us
  local copies, waits for them, and re-layouts: 107 us -> 2.14 us
  Pallas kernels: 0 us -> 34.6 us
  waiting for transfers between devices: 71 us -> 97.5 us
  other arithmetic: 22.7 us -> 0 us
  between operations: 13.6 us -> 0.04 us
  matrix products: 12 us -> 4.4 us
  starting transfers between devices: 18.6 us -> 22.9 us
    psum x1 -> x0, blocking collectives: 122 us -> none  [per_device(): total_sums, counts = lax.psum((sums, counts), 'seq')]
    all_to_all x3, waiting for transfers between devices: 25.1 us -> 97.4 us  [the longest x1 47.5 us: per_device(): received_kv = exchange(send_kv)]
    unnamed x25 -> x4, local copies, waits for them, and re-layouts: 44.8 us -> 1.03 us
    pallas_call x0 -> x6, Pallas kernels: none -> 34.6 us  [the longest x1 9.5 us: per_device(): pl.pallas_call(functools.partial(attend_kernel, rows, cap), grid=(heads /...]
    psum x1 -> x0, waiting for transfers between devices: 34.5 us -> none  [per_device(): total_sums, counts = lax.psum((sums, counts), 'seq')]
    gather x2 -> x0, local copies, waits for them, and re-layouts: 18.9 us -> none  [per_device(): picked = jnp.take_along_axis(flat, place[:, :, None], axis=1)]
    reshape x8 -> x0, local copies, waits for them, and re-layouts: 18 us -> none  [the longest x2 11.7 us: per_device(): buffer = buffer.reshape(heads, clusters, cap, 3 * head_dim)]
    reduce_scatter x1 -> x0, waiting for transfers between devices: 11.4 us -> none  [per_device(): lax.psum_scatter(partial_out, 'head', scatter_dimension=1, tiled=True)]
  transfers between devices with their start and end apart: 5 -> 5, of which waited for: 3 -> 4; matrix products, arithmetic and copies ran while one was open for 13% -> 2% of each run, Pallas kernels for 0% -> 10%
where the time goes in v2:
time: 162 us
  waiting for transfers between devices  97.5 us (60%)
  Pallas kernels  34.6 us (21%)
  starting transfers between devices  22.9 us (14%)
  matrix products  4.4 us (3%)
  local copies, waits for them, and re-layouts  2.14 us (1%)
    all_to_all x1, waiting for transfers between devices, per_device(): received_kv = exchange(send_kv)  47.5 us
    all_to_all x1, waiting for transfers between devices, per_device(): received_q = exchange(send_q)  25.9 us
    all_to_all x1, waiting for transfers between devices, per_device(): returned = exchange(answers)  24 us
    pallas_call x1, Pallas kernels, per_device(): pl.pallas_call(functools.partial(attend_kernel, rows, cap), grid=(heads /...  9.5 us
    pallas_call x1, Pallas kernels, per_device(): pl.pallas_call(functools.partial(regroup_kernel, rows, cap), grid=(heads,...  7.25 us
    all_to_all x1, starting transfers between devices, per_device(): received_kv = exchange(send_kv)  6.66 us
    all_to_all x1, starting transfers between devices, per_device(): received_q = exchange(send_q)  6.62 us
    pallas_call x1, Pallas kernels, per_device(): pl.pallas_call(functools.partial(pack_kv_kernel, rows, cap), grid=(heads...  5.7 us
  transfers between devices with their start and end apart: 5, of which 4 were waited for; matrix products, arithmetic and copies ran while one was open for 2% of the time, Pallas kernels for 10%

profile of v2, /device:TPU:9, one launch (start us, length us, event | category | flops | bytes accessed | tf_op | source)
XLA Modules:
  0.0 161.6 jit_solution(7464649278535930758)
XLA Ops:
  0.0 0.0 copy-start
  0.0 5.7 %pack_kv.1 = (bf16[16,6,48,256]{3,2,1,0:T(8,128)(2,1)}, s32[6,1,384]{2,1,0:T(1,128)}) custom-call(s32[6,1,384]{2,1,0:T(1,128)} %bitcast.5, bf16[384,768]{1,0:T(8,128)(2,1)} %k_ref.1, bf16[384,768]{1,0:T(8,128)(2,1)} %v_ref.1), custom_call_target="tpu_custom_call" | custom-call | tf_op jit(solution)/shard_map/pack_kv/pallas_call | solution.py:282
  5.7 6.7 %all-to-all-start = ((bf16[16,6,48,256]{3,2,1,0:T(8,128)(2,1)}), bf16[16,6,48,256]{3,2,1,0:T(8,128)(2,1)}, u32[]{:S(2)}, u32[]{:S(2)}) async-start(bf16[16,6,48,256]{3,2,1,0:T(8,128)(2,1)} %get-tuple-element.13), calls=%async_computation | async-start | bytes 4718592 | tf_op jit(solution)/shard_map/all_to_all | solution.py:292
  12.4 3.8 %pack_q.1 = (bf16[16,352,128]{2,1,0:T(8,128)(2,1)}, s32[384,128]{1,0:T(8,128)}) custom-call(s32[6,1,384]{2,1,0:T(1,128)} %get-tuple-element.11.place_ref, bf16[384,768]{1,0:T(8,128)(2,1)} %q_ref.1), custom_call_target="tpu_custom_call" | custom-call | tf_op jit(solution)/shard_map/pack_q/pallas_call | solution.py:297
  16.2 47.5 %all-to-all-done.recv_ref = bf16[16,6,48,256]{3,2,1,0:T(8,128)(2,1)} async-done(((bf16[16,6,48,256]{3,2,1,0:T(8,128)(2,1)}), bf16[16,6,48,256]{3,2,1,0:T(8,128)(2,1)}, u32[]{:S(2)}, u32[]{:S(2)}) %all-to-all-start) | async-done | bytes 2359328 | tf_op jit(solution)/shard_map/all_to_all | solution.py:292
  63.7 4.1 %centers.1 = bf16[16,352,128]{2,1,0:T(8,128)(2,1)} custom-call(bf16[16,6,48,256]{3,2,1,0:T(8,128)(2,1)} %all-to-all-done.recv_ref, bf16[16,352,128]{2,1,0:T(8,128)(2,1)} %get-tuple-element.14.buffer_ref), custom_call_target="tpu_custom_call", output_to_operand_aliasing={{}: (1, {})} | custom-call | tf_op jit(solution)/shard_map/centers/pallas_call | solution.py:308
  67.8 6.6 %all-to-all-start.1 = ((bf16[16,352,128]{2,1,0:T(8,128)(2,1)}), bf16[16,352,128]{2,1,0:T(8,128)(2,1)}, u32[]{:S(2)}, u32[]{:S(2)}) async-start(bf16[16,352,128]{2,1,0:T(8,128)(2,1)} %centers.1), calls=%async_computation.1 | async-start | bytes 2883584 | tf_op jit(solution)/shard_map/all_to_all | solution.py:324
  74.4 7.2 %regroup.1 = (bf16[6,4,192,256]{3,2,1,0:T(8,128)(2,1)}, bf16[6,4,192,256]{3,2,1,0:T(8,128)(2,1)}) custom-call(bf16[16,6,48,256]{3,2,1,0:T(8,128)(2,1)} %all-to-all-done.recv_ref), custom_call_target="tpu_custom_call" | custom-call | tf_op jit(solution)/shard_map/regroup/pallas_call | solution.py:330
  81.6 25.9 %all-to-all-done.1.recv_ref = bf16[16,352,128]{2,1,0:T(8,128)(2,1)} async-done(((bf16[16,352,128]{2,1,0:T(8,128)(2,1)}), bf16[16,352,128]{2,1,0:T(8,128)(2,1)}, u32[]{:S(2)}, u32[]{:S(2)}) %all-to-all-start.1) | async-done | bytes 1441824 | tf_op jit(solution)/shard_map/all_to_all | solution.py:324
  107.5 9.5 %attend.1 = bf16[16,6,48,128]{3,2,1,0:T(8,128)(2,1)} custom-call(s32[1]{0:T(128)} %bitcast.1.rank_ref, bf16[16,352,128]{2,1,0:T(8,128)(2,1)} %all-to-all-done.1.recv_ref, bf16[6,4,192,256]{3,2,1,0:T(8,128)(2,1)} %get-tuple-element.15.near_key_ref, bf16[6,4,192,256]{3,2,1,0:T(8,128)(2,1)} %get-tuple-element.16.near_value_ref), custom_call_target="tpu_custom_call" | custom-call | tf_op jit(solution)/shard_map/attend/pallas_call | solution.py:341
  117.0 5.0 %all-to-all-start.2 = ((bf16[16,6,48,128]{3,2,1,0:T(8,128)(2,1)}), bf16[16,6,48,128]{3,2,1,0:T(8,128)(2,1)S(1)}, u32[]{:S(2)}, u32[]{:S(2)}) async-start(bf16[16,6,48,128]{3,2,1,0:T(8,128)(2,1)} %attend.1), calls=%async_computation.2 | async-start | bytes 2359296 | tf_op jit(solution)/shard_map/all_to_all | solution.py:359
  122.0 0.0 copy-done
  122.0 1.1 constant_dynamic-slice_fusion
  123.1 2.0 %collective-permute-start.1 = (bf16[768,768]{1,0:T(8,128)(2,1)}, bf16[768,768]{1,0:T(8,128)(2,1)}, u32[]{:S(2)}, u32[]{:S(2)}) collective-permute-start(bf16[768,768]{1,0:T(8,128)(2,1)} %constant_dynamic-slice_fusion), channel_id=1, source_target_pairs={{0,1},{1,0},{2,3},{3,2},{4,5},{5,4},{6,7},{7,6},{8,9},{9,8},{10,11... | collective-permute-start | bytes 3538952 | tf_op jit(solution)/shard_map/ppermute | solution.py:270
  125.2 24.0 %all-to-all-done.2.back_ref = bf16[16,6,48,128]{3,2,1,0:T(8,128)(2,1)S(1)} async-done(((bf16[16,6,48,128]{3,2,1,0:T(8,128)(2,1)}), bf16[16,6,48,128]{3,2,1,0:T(8,128)(2,1)S(1)}, u32[]{:S(2)}, u32[]{:S(2)}) %all-to-all-start.2) | async-done | bytes 1179680 | tf_op jit(solution)/shard_map/all_to_all | solution.py:359
  149.2 0.0 copy-start.1
  149.2 1.0 copy-done.1
  150.2 4.3 %unpack.1 = bf16[384,768]{1,0:T(8,128)(2,1)} custom-call(s32[384,128]{1,0:T(8,128)} %get-tuple-element.12.column_ref, bf16[16,6,48,128]{3,2,1,0:T(8,128)(2,1)} %copy-done.1), custom_call_target="tpu_custom_call" | custom-call | tf_op jit(solution)/shard_map/unpack/pallas_call | solution.py:361
  154.5 2.5 %collective-permute-start = (bf16[384,768]{1,0:T(8,128)(2,1)}, bf16[384,768]{1,0:T(8,128)(2,1)S(1)}, u32[]{:S(2)}, u32[]{:S(2)}) collective-permute-start(bf16[384,768]{1,0:T(8,128)(2,1)} %unpack.1), channel_id=1, source_target_pairs={{0,1},{1,0},{2,3},{3,2},{4,5},{5,4},{6,7},{7,6},{8,9},{9,8},{10,11... | collective-permute-start | bytes 1769480 | tf_op jit(solution)/shard_map/ppermute | solution.py:370
  157.0 1.7 %fusion.1 = f32[384,768]{1,0:T(8,128)S(1)} fusion(bf16[384,768]{1,0:T(8,128)(2,1)} %unpack.1, bf16[768,1536]{1,0:T(8,128)(2,1)S(1)} %copy-done, s32[]{:T(128)S(6)} %select_n.6), kind=kOutput, calls=%fused_computation.2 | convolution fusion | flops 452984832 | bytes 2949124 | tf_op jit(solution)/shard_map/dot_general | solution.py:27
  158.7 0.0 collective-permute-done.1
  158.7 0.1 collective-permute-done
  158.9 2.7 %fusion = bf16[384,768]{1,0:T(8,128)(2,1)} fusion(f32[384,768]{1,0:T(8,128)S(1)} %fusion.1, bf16[384,768]{1,0:T(8,128)(2,1)S(1)} %collective-permute-done, bf16[768,768]{1,0:T(8,128)(2,1)} %collective-permute-done.1), kind=kOutput, calls=%fused_computation.1 | convolution fusion | flops 453574656 | bytes 3538944 | tf_op jit(solution)/shard_map/dot_general | solution.py:27
Async XLA Ops:
  0.0 122.0 %copy-start = (bf16[768,1536]{1,0:T(8,128)(2,1)S(1)}, bf16[768,1536]{1,0:T(8,128)(2,1)}, u32[]{:S(2)}) copy-start(bf16[768,1536]{1,0:T(8,128)(2,1)} %param.9) | copy-start | bytes 7077892
  5.7 58.0 %all-to-all-start = ((bf16[16,6,48,256]{3,2,1,0:T(8,128)(2,1)}), bf16[16,6,48,256]{3,2,1,0:T(8,128)(2,1)}, u32[]{:S(2)}, u32[]{:S(2)}) async-start(bf16[16,6,48,256]{3,2,1,0:T(8,128)(2,1)} %get-tuple-element.13), calls=%async_computation | async-start | bytes 4718592 | tf_op jit(solution)/shard_map/all_to_all | solution.py:292
  67.8 39.7 %all-to-all-start.1 = ((bf16[16,352,128]{2,1,0:T(8,128)(2,1)}), bf16[16,352,128]{2,1,0:T(8,128)(2,1)}, u32[]{:S(2)}, u32[]{:S(2)}) async-start(bf16[16,352,128]{2,1,0:T(8,128)(2,1)} %centers.1), calls=%async_computation.1 | async-start | bytes 2883584 | tf_op jit(solution)/shard_map/all_to_all | solution.py:324
  117.0 32.2 %all-to-all-start.2 = ((bf16[16,6,48,128]{3,2,1,0:T(8,128)(2,1)}), bf16[16,6,48,128]{3,2,1,0:T(8,128)(2,1)S(1)}, u32[]{:S(2)}, u32[]{:S(2)}) async-start(bf16[16,6,48,128]{3,2,1,0:T(8,128)(2,1)} %attend.1), calls=%async_computation.2 | async-start | bytes 2359296 | tf_op jit(solution)/shard_map/all_to_all | solution.py:359
  123.1 35.6 %collective-permute-start.1 = (bf16[768,768]{1,0:T(8,128)(2,1)}, bf16[768,768]{1,0:T(8,128)(2,1)}, u32[]{:S(2)}, u32[]{:S(2)}) collective-permute-start(bf16[768,768]{1,0:T(8,128)(2,1)} %constant_dynamic-slice_fusion), channel_id=1, source_target_pairs={{0,1},{1,0},{2,3},{3,2},{4,5},{5,4},{6,7},{7,6},{8,9},{9,8},{10,11... | collective-permute-start | bytes 3538952 | tf_op jit(solution)/shard_map/ppermute | solution.py:270
  149.2 1.0 copy-start.1
  154.5 4.4 %collective-permute-start = (bf16[384,768]{1,0:T(8,128)(2,1)}, bf16[384,768]{1,0:T(8,128)(2,1)S(1)}, u32[]{:S(2)}, u32[]{:S(2)}) collective-permute-start(bf16[384,768]{1,0:T(8,128)(2,1)} %unpack.1), channel_id=1, source_target_pairs={{0,1},{1,0},{2,3},{3,2},{4,5},{5,4},{6,7},{7,6},{8,9},{9,8},{10,11... | collective-permute-start | bytes 1769480 | tf_op jit(solution)/shard_map/ppermute | solution.py:370

commit v3 on v2

v3 whole, which is shorter than its diff:
```python
import functools
import math

import jax
import jax.numpy as jnp
from jax import lax
from jax.experimental import pallas as pl
from jax.experimental.pallas import tpu as pltpu
from jax.sharding import PartitionSpec as P

CL_DEV = 4
NEG = -1e30
EMPTY = 128.0
BF16 = jnp.bfloat16
F32 = jnp.float32


def iota(shape, dim):
    return lax.broadcasted_iota(jnp.int32, shape, dim)


def nt_dot(a, b):
    return lax.dot_general(a, b, (((1,), (1,)), ((), ())), preferred_element_type=F32)


def nn_dot(a, b):
    return jnp.dot(a, b, preferred_element_type=F32)


def one_zero(mask, kind=BF16):
    return jnp.where(mask, 1.0, 0.0).astype(kind)


def pack_kv_kernel(rows, cap, member_ref, k_ref, v_ref, send_ref, place_ref, lower_ref):
    tok = k_ref.shape[0]
    n_seq, per_step = send_ref.shape[:2]
    hd = k_ref.shape[1] // per_step
    slots = n_seq * rows
    clusters = n_seq * CL_DEV

    @pl.when(pl.program_id(0) == 0)
    def _():
        lower_ref[...] = one_zero(iota((tok, tok), 0) < iota((tok, tok), 1))

    for i in range(per_step):
        member = member_ref[i]
        same = iota((clusters, tok), 0) == member
        before = nn_dot(one_zero(same), lower_ref[...])
        slot = jnp.sum(jnp.where(same, before, 0.0), axis=0, keepdims=True).astype(jnp.int32)
        place = (member // CL_DEV) * rows + (member % CL_DEV) * cap + slot
        place_ref[i] = place
        hot = one_zero(iota((slots, tok), 0) == place, F32)
        live = jnp.sum(hot, axis=1, keepdims=True)
        span = slice(i * hd, (i + 1) * hd)
        pair = jnp.concatenate([k_ref[:, span], v_ref[:, span]], 1)
        packed = nn_dot(hot.astype(BF16), pair)
        mark = jnp.where(iota((slots, hd), 1) == 0, EMPTY * (1.0 - live), 0.0)
        key = (packed[:, :hd] + mark).astype(BF16)
        send_ref[:, i, :, :hd] = key.reshape(n_seq, rows, hd)
        send_ref[:, i, :, hd:] = packed[:, hd:].astype(BF16).reshape(n_seq, rows, hd)


def pack_q_kernel(rows, place_ref, q_ref, send_ref, column_ref):
    tok = q_ref.shape[0]
    n_seq = send_ref.shape[0]
    per_step = send_ref.shape[1] // rows
    hd = q_ref.shape[1] // per_step
    slots = n_seq * rows
    h = pl.program_id(0) * per_step

    @pl.when(h == 0)
    def _():
        column_ref[...] = jnp.zeros_like(column_ref)

    for i in range(per_step):
        place = place_ref[i]
        hot = one_zero(iota((slots, tok), 0) == place)
        packed = nn_dot(hot, q_ref[:, i * hd : (i + 1) * hd])
        send_ref[:, i * rows : (i + 1) * rows] = packed.astype(BF16).reshape(n_seq, rows, hd)
        turned = jnp.broadcast_to(place.astype(F32), (128, tok)).T.astype(jnp.int32)
        column_ref[...] += jnp.where(iota((tok, 128), 1) == h + i, turned, 0)


def regroup_kernel(rows, cap, recv_ref, pair_ref, perm_ref):
    h = pl.program_id(0)
    n_seq = recv_ref.shape[0]
    slots = n_seq * rows
    near = n_seq * cap

    @pl.when(h == 0)
    def _():
        line = iota((near, 1), 0)
        source = line // cap
        origin = source * rows + (line - source * cap)
        for e in range(CL_DEV):
            perm_ref[e] = one_zero(iota((near, slots), 1) == origin + e * cap)

    pairs = recv_ref[:, 0].reshape(slots, recv_ref.shape[3])
    for e in range(CL_DEV):
        pair_ref[0, e] = nn_dot(perm_ref[e], pairs).astype(BF16)


def centers_kernel(cap, recv_ref, buffer_ref, send_ref, block_ref, sem):
    del buffer_ref
    n_seq, heads, rows, _ = recv_ref.shape
    _, extra, hd = block_ref.shape
    owned = heads * CL_DEV
    row = iota((rows, 1), 0)
    line = iota((extra, 1), 0)
    total = jnp.zeros((extra, hd), F32)
    count = jnp.zeros((extra, 1), F32)
    for h in range(heads):
        key = recv_ref[:, h, :, :hd].astype(F32)
        value = jnp.sum(recv_ref[:, h, :, hd:].astype(F32), axis=0)
        empty = key > 0.5 * EMPTY
        key = jnp.sum(jnp.where(empty, 0.0, key), axis=0)
        number = n_seq - jnp.sum(jnp.where(empty, 1.0, 0.0), axis=0)[:, :1]
        for e in range(CL_DEV):
            inside = (row >= e * cap) & (row < (e + 1) * cap)
            key_sum = jnp.sum(jnp.where(inside, key, 0.0), axis=0, keepdims=True)
            value_sum = jnp.sum(jnp.where(inside, value, 0.0), axis=0, keepdims=True)
            amount = jnp.sum(jnp.where(inside, number, 0.0), axis=0, keepdims=True)
            here, there = line == h * CL_DEV + e, line == h * CL_DEV + e + owned
            total = jnp.where(here, key_sum, jnp.where(there, value_sum, total))
            count = jnp.where(here | there, amount, count)
    centers = total / jnp.maximum(count, 1.0)
    r, l = iota((extra, hd), 0), iota((extra, hd), 1)
    diagonal = jnp.sum(jnp.where(r == l, count, 0.0), axis=0, keepdims=True)
    block = jnp.where(r == 2 * owned, diagonal, centers).astype(BF16)
    for j in range(n_seq):
        block_ref[j] = block
    copy = pltpu.make_async_copy(block_ref, send_ref.at[:, pl.ds(heads * rows, extra)], sem)
    copy.start()
    copy.wait()


def prepare_far(rank, all_centers, heads, key_ref, value_ref):
    _, far, _ = value_ref.shape
    n_seq, block, hd = all_centers.shape
    owned = heads * CL_DEV
    root = math.sqrt(hd)
    everything = all_centers.reshape(n_seq * block, hd)
    line = iota((far, 1), 0)
    base = (line // CL_DEV) * block
    cluster = line % CL_DEV

    def rows_at(offsets):
        wanted = jnp.concatenate([base + offset for offset in offsets], 0)
        return nn_dot(one_zero(iota((wanted.shape[0], n_seq * block), 1) == wanted), everything)

    counts = rows_at([2 * owned])
    offsets = [part * owned + h * CL_DEV + cluster for h in range(heads) for part in range(2)]
    if n_seq <= 16:
        means = rows_at(offsets)
        means = [means[i * far : (i + 1) * far] for i in range(len(offsets))]
    else:
        means = [rows_at([offset]) for offset in offsets]
    lane = iota((far, hd), 1)
    own = (line // CL_DEV == rank) & (lane == cluster + 3)
    for h in range(heads):
        count = jnp.sum(
            jnp.where(lane == cluster + h * CL_DEV, counts, 0.0), axis=1, keepdims=True
        )
        bias = jnp.where(count > 0, jnp.log(jnp.maximum(count, 1.0)) * root, NEG)
        high = bias.astype(BF16).astype(F32)
        middle = (bias - high).astype(BF16).astype(F32)
        low = bias - high - middle
        side = jnp.where(lane == 0, high, jnp.where(lane == 1, middle, jnp.where(lane == 2, low, 0.0)))
        side = jnp.where(own, NEG, side)
        key_ref[h, :, :hd] = means[2 * h].astype(BF16)
        key_ref[h, :, hd:] = side.astype(BF16)
        value_ref[h, :, :hd] = means[2 * h + 1].astype(BF16)
        value_ref[h, :, hd:] = jnp.ones((far, hd), BF16)


def tile_clusters(tile, rows, cap):
    ends = [(e + 1) * cap for e in range(CL_DEV - 1)] + [rows]
    return [e for e in range(CL_DEV) if e * cap < tile * 16 + 16 and ends[e] > tile * 16]


def attend_kernel(
    cap, rank_ref, q_ref, near_ref, out_ref,
    far_key_ref, far_value_ref, mask_ref, side_ref,
):
    step = pl.program_id(0)
    n_seq, per_step, rows, hd = out_ref.shape
    heads = far_key_ref.shape[0]
    group = n_seq * 16
    tiles = [tile_clusters(tile, rows, cap) for tile in range(rows // 16)]

    @pl.when(step == 0)
    def _():
        lane = iota((group, hd), 1)
        row = lax.rem(iota((group, hd), 0), 16)
        for tile, clusters in enumerate(tiles):
            place = row + tile * 16
            for j, e in enumerate(clusters):
                inside = place >= e * cap
                if e + 1 < CL_DEV:
                    inside = inside & (place < (e + 1) * cap)
                mask_ref[tile, j] = one_zero(inside)
                side_ref[tile, j] = one_zero(inside & ((lane < 3) | (lane == 3 + e)))
        prepare_far(rank_ref[0], q_ref[:, heads * rows :], heads, far_key_ref, far_value_ref)

    scale = math.log2(math.e) / math.sqrt(hd)
    for i in range(per_step):
        h = step * per_step + i
        far_key, far_value = far_key_ref[h], far_value_ref[h]
        keys, values = [], []
        for e in range(CL_DEV):
            key, value = near_ref[i, e, :, :hd], near_ref[i, e, :, hd:]
            side = jnp.where(key > 0.5 * EMPTY, NEG, 0.0).astype(BF16)
            keys.append(jnp.concatenate([jnp.concatenate([key, side], 1), far_key], 0))
            ones = jnp.ones(value.shape, BF16)
            values.append(jnp.concatenate([jnp.concatenate([value, ones], 1), far_value], 0))
        for tile, clusters in enumerate(tiles):
            start = pl.multiple_of(h * rows + tile * 16, 16)
            query = q_ref[:, pl.ds(start, 16)].reshape(group, hd)
            wide = []
            for j in range(len(clusters)):
                wide += [query * mask_ref[tile, j], side_ref[tile, j]]
            wide = jnp.concatenate(wide, 1)
            score = nt_dot(wide, jnp.concatenate([keys[e] for e in clusters], 1))
            top = jnp.max(score, 1, keepdims=True)
            weight = jnp.exp2((score - top) * scale).astype(BF16)
            repeat = weight.shape[1] // hd
            wide = [weight * jnp.concatenate([mask_ref[tile, j]] * repeat, 1) for j in range(len(clusters))]
            wide = jnp.concatenate(wide, 1)
            mixed = nn_dot(wide, jnp.concatenate([values[e] for e in clusters], 0))
            total = mixed[:, hd:]
            inverse = pl.reciprocal(total, approx=True)
            inverse = inverse * (2.0 - total * inverse)
            answer = (mixed[:, :hd] * inverse).astype(BF16)
            out_ref[:, i, tile * 16 : tile * 16 + 16] = answer.reshape(n_seq, 16, hd)


def unpack_kernel(column_ref, back_ref, out_ref):
    n_seq, per_step, rows, hd = back_ref.shape
    tok = out_ref.shape[0]
    slots = n_seq * rows
    h = pl.program_id(0) * per_step
    column = column_ref[...]
    for i in range(per_step):
        place = jnp.sum(
            jnp.where(iota((tok, 128), 1) == h + i, column, 0), axis=1, keepdims=True
        )
        hot = one_zero(iota((tok, slots), 1) == place)
        answer = nn_dot(hot, back_ref[:, i].reshape(slots, hd))
        out_ref[:, i * hd : (i + 1) * hd] = answer.astype(BF16)


def per_device(queries, keys, values, membership, w_out):
    n_seq = lax.axis_size("seq")
    groups = lax.axis_size("head")
    rank = lax.axis_index("seq")
    group = lax.axis_index("head")
    tok = queries.shape[0]
    heads = membership.shape[0]
    hd = queries.shape[1] // heads
    width = w_out.shape[1] // groups
    clusters = CL_DEV * n_seq
    cap = max(2, (2 * tok + clusters - 1) // clusters)
    rows = (CL_DEV * cap + 15) // 16 * 16
    near = n_seq * cap
    per_step = 2
    params = pltpu.CompilerParams(
        dimension_semantics=("arbitrary",),
        vmem_limit_bytes=60 * 1024 * 1024,
    )
    small = pltpu.CompilerParams(
        dimension_semantics=("arbitrary",),
        vmem_limit_bytes=(16 if n_seq <= 16 else 60) * 1024 * 1024,
    )
    exchange = functools.partial(
        lax.all_to_all, axis_name="seq", split_axis=0, concat_axis=0, tiled=True
    )
    swap = [(i, (i + 1) % groups) for i in range(groups)]

    mine = lax.dynamic_slice_in_dim(w_out, group * width, width, 1)
    other = lax.dynamic_slice_in_dim(w_out, (1 - group) * width, width, 1)
    other = lax.ppermute(other, "head", swap)

    matrix = pl.BlockSpec((tok, per_step * hd), lambda h: (0, h))
    line = pl.BlockSpec((per_step, 1, tok), lambda h: (h, 0, 0))
    column = pl.BlockSpec((tok, 128), lambda h: (0, 0))

    def slot_block(depth, count):
        return pl.BlockSpec((n_seq, count, rows, depth), lambda h: (0, h, 0, 0))

    def slot_array(depth):
        return jax.ShapeDtypeStruct((n_seq, heads, rows, depth), BF16)

    send_kv, place = pl.pallas_call(
        functools.partial(pack_kv_kernel, rows, cap),
        grid=(heads // per_step,),
        in_specs=[line, matrix, matrix],
        out_specs=[slot_block(2 * hd, per_step), line],
        out_shape=[slot_array(2 * hd), jax.ShapeDtypeStruct((heads, 1, tok), jnp.int32)],
        scratch_shapes=[pltpu.VMEM((tok, tok), BF16)],
        compiler_params=params,
        name="pack_kv",
    )(membership.reshape(heads, 1, tok), keys, values)
    received_kv = exchange(send_kv)

    extra = (2 * heads * CL_DEV + 1 + 31) // 32 * 32
    all_rows = heads * rows + extra
    q_array = jax.ShapeDtypeStruct((n_seq, all_rows, hd), BF16)
    q_block = pl.BlockSpec((n_seq, per_step * rows, hd), lambda h: (0, h, 0))
    send_q, columns = pl.pallas_call(
        functools.partial(pack_q_kernel, rows),
        grid=(heads // per_step,),
        in_specs=[line, matrix],
        out_specs=[q_block, column],
        out_shape=[q_array, jax.ShapeDtypeStruct((tok, 128), jnp.int32)],
        compiler_params=params,
        name="pack_q",
    )(place, queries)

    anywhere = pl.BlockSpec(memory_space=pl.ANY)
    in_vmem = pl.BlockSpec(memory_space=pltpu.VMEM)
    send_q = pl.pallas_call(
        functools.partial(centers_kernel, cap),
        in_specs=[in_vmem, anywhere],
        out_specs=anywhere,
        out_shape=q_array,
        scratch_shapes=[
            pltpu.VMEM((n_seq, extra, hd), BF16),
            pltpu.SemaphoreType.DMA,
        ],
        input_output_aliases={1: 0},
        compiler_params=pltpu.CompilerParams(vmem_limit_bytes=params.vmem_limit_bytes),
        name="centers",
    )(received_kv, send_q)
    received_q = exchange(send_q)

    def near_block(count):
        return pl.BlockSpec((count, CL_DEV, near, 2 * hd), lambda h: (h, 0, 0, 0))

    near_pairs = pl.pallas_call(
        functools.partial(regroup_kernel, rows, cap),
        grid=(heads,),
        in_specs=[slot_block(2 * hd, 1)],
        out_specs=near_block(1),
        out_shape=jax.ShapeDtypeStruct((heads, CL_DEV, near, 2 * hd), BF16),
        scratch_shapes=[pltpu.VMEM((CL_DEV, near, n_seq * rows), BF16)],
        compiler_params=params,
        name="regroup",
    )(received_kv)

    many = 3
    answers = pl.pallas_call(
        functools.partial(attend_kernel, cap),
        grid=(heads // many,),
        in_specs=[pl.BlockSpec(memory_space=pltpu.SMEM), in_vmem, near_block(many)],
        out_specs=slot_block(hd, many),
        out_shape=slot_array(hd),
        scratch_shapes=[
            pltpu.VMEM((heads, clusters, 2 * hd), BF16),
            pltpu.VMEM((heads, clusters, 2 * hd), BF16),
            pltpu.VMEM((rows // 16, CL_DEV, n_seq * 16, hd), BF16),
            pltpu.VMEM((rows // 16, CL_DEV, n_seq * 16, hd), BF16),
        ],
        compiler_params=params,
        name="attend",
    )(rank.reshape(1), received_q, near_pairs)
    returned = exchange(answers)

    attended = pl.pallas_call(
        unpack_kernel,
        grid=(heads // per_step,),
        in_specs=[column, slot_block(hd, per_step)],
        out_specs=matrix,
        out_shape=jax.ShapeDtypeStruct((tok, heads * hd), BF16),
        compiler_params=small,
        name="unpack",
    )(columns, returned)
    partner = lax.ppermute(attended, "head", swap)
    result = nn_dot(attended, mine) + nn_dot(partner, other)
    return result.astype(BF16)


def solution(mesh):
    return jax.shard_map(
        per_device,
        mesh=mesh,
        in_specs=(
            P("seq", "head"),
            P("seq", "head"),
            P("seq", "head"),
            P("head", "seq", None),
            P("head", None),
        ),
        out_specs=P("seq", "head"),
        check_vma=False,
    )
```

time: 162 us -> 158 us (0.975)
  Pallas kernels: 34.6 us -> 29.5 us
    pallas_call x2, Pallas kernels: 13.6 us -> 10.9 us  [the longest x1 7.36 us: per_device(): pl.pallas_call(functools.partial(attend_kernel, cap), grid=(heads // many...]
  transfers between devices with their start and end apart: 5 -> 5, of which waited for: 4 -> 4; matrix products, arithmetic and copies ran while one was open for 2% -> 2% of each run, Pallas kernels for 10% -> 8%
where the time goes in v3:
time: 158 us; the launch traced here: 157 us
  waiting for transfers between devices  98.4 us (62%)
  Pallas kernels  29.5 us (19%)
  starting transfers between devices  22.9 us (14%)
  matrix products  4.4 us (3%)
  local copies, waits for them, and re-layouts  2.04 us (1%)
    all_to_all x1, waiting for transfers between devices, per_device(): received_kv = exchange(send_kv)  47.5 us
    all_to_all x1, waiting for transfers between devices, per_device(): received_q = exchange(send_q)  26.7 us
    all_to_all x1, waiting for transfers between devices, per_device(): returned = exchange(answers)  24 us
    pallas_call x1, Pallas kernels, per_device(): pl.pallas_call(functools.partial(attend_kernel, cap), grid=(heads // many...  7.36 us
    all_to_all x1, starting transfers between devices, per_device(): received_kv = exchange(send_kv)  6.66 us
    all_to_all x1, starting transfers between devices, per_device(): received_q = exchange(send_q)  6.62 us
    pallas_call x1, Pallas kernels, per_device(): pl.pallas_call(functools.partial(regroup_kernel, rows, cap), grid=(heads,...  6.37 us
    pallas_call x1, Pallas kernels, per_device(): pl.pallas_call(functools.partial(pack_kv_kernel, rows, cap), grid=(heads...  5.42 us
  transfers between devices with their start and end apart: 5, of which 4 were waited for; matrix products, arithmetic and copies ran while one was open for 2% of the time, Pallas kernels for 8%

profile of v3, /device:TPU:9, one launch (start us, length us, event | category | flops | bytes accessed | tf_op | source)
XLA Modules:
  0.0 157.3 jit_solution(9590599899860780639)
XLA Ops:
  0.0 0.0 copy-start
  0.0 5.4 %pack_kv.1 = (bf16[16,6,48,256]{3,2,1,0:T(8,128)(2,1)}, s32[6,1,384]{2,1,0:T(1,128)}) custom-call(s32[6,1,384]{2,1,0:T(1,128)} %bitcast.5, bf16[384,768]{1,0:T(8,128)(2,1)} %k_ref.1, bf16[384,768]{1,0:T(8,128)(2,1)} %v_ref.1), custom_call_target="tpu_custom_call" | custom-call | tf_op jit(solution)/shard_map/pack_kv/pallas_call | solution.py:293
  5.4 6.7 %all-to-all-start = ((bf16[16,6,48,256]{3,2,1,0:T(8,128)(2,1)}), bf16[16,6,48,256]{3,2,1,0:T(8,128)(2,1)}, u32[]{:S(2)}, u32[]{:S(2)}) async-start(bf16[16,6,48,256]{3,2,1,0:T(8,128)(2,1)} %get-tuple-element.11), calls=%async_computation | async-start | bytes 4718592 | tf_op jit(solution)/shard_map/all_to_all | solution.py:303
  12.1 3.8 %pack_q.1 = (bf16[16,352,128]{2,1,0:T(8,128)(2,1)}, s32[384,128]{1,0:T(8,128)}) custom-call(s32[6,1,384]{2,1,0:T(1,128)} %get-tuple-element.9.place_ref, bf16[384,768]{1,0:T(8,128)(2,1)} %q_ref.1), custom_call_target="tpu_custom_call" | custom-call | tf_op jit(solution)/shard_map/pack_q/pallas_call | solution.py:309
  15.9 47.5 %all-to-all-done.recv_ref = bf16[16,6,48,256]{3,2,1,0:T(8,128)(2,1)} async-done(((bf16[16,6,48,256]{3,2,1,0:T(8,128)(2,1)}), bf16[16,6,48,256]{3,2,1,0:T(8,128)(2,1)}, u32[]{:S(2)}, u32[]{:S(2)}) %all-to-all-start) | async-done | bytes 2359328 | tf_op jit(solution)/shard_map/all_to_all | solution.py:303
  63.4 3.5 %centers.1 = bf16[16,352,128]{2,1,0:T(8,128)(2,1)} custom-call(bf16[16,6,48,256]{3,2,1,0:T(8,128)(2,1)} %all-to-all-done.recv_ref, bf16[16,352,128]{2,1,0:T(8,128)(2,1)} %get-tuple-element.12.buffer_ref), custom_call_target="tpu_custom_call", output_to_operand_aliasing={{}: (1, {})} | custom-call | tf_op jit(solution)/shard_map/centers/pallas_call | solution.py:321
  67.0 6.6 %all-to-all-start.1 = ((bf16[16,352,128]{2,1,0:T(8,128)(2,1)}), bf16[16,352,128]{2,1,0:T(8,128)(2,1)}, u32[]{:S(2)}, u32[]{:S(2)}) async-start(bf16[16,352,128]{2,1,0:T(8,128)(2,1)} %centers.1), calls=%async_computation.1 | async-start | bytes 2883584 | tf_op jit(solution)/shard_map/all_to_all | solution.py:334
  73.6 6.4 %regroup.1.near_ref = bf16[6,4,192,256]{3,2,1,0:T(8,128)(2,1)} custom-call(bf16[16,6,48,256]{3,2,1,0:T(8,128)(2,1)} %all-to-all-done.recv_ref), custom_call_target="tpu_custom_call" | custom-call | tf_op jit(solution)/shard_map/regroup/pallas_call | solution.py:339
  80.0 26.7 %all-to-all-done.1.q_ref = bf16[16,352,128]{2,1,0:T(8,128)(2,1)} async-done(((bf16[16,352,128]{2,1,0:T(8,128)(2,1)}), bf16[16,352,128]{2,1,0:T(8,128)(2,1)}, u32[]{:S(2)}, u32[]{:S(2)}) %all-to-all-start.1) | async-done | bytes 1441824 | tf_op jit(solution)/shard_map/all_to_all | solution.py:334
  106.7 7.4 %attend.1 = bf16[16,6,48,128]{3,2,1,0:T(8,128)(2,1)} custom-call(s32[1]{0:T(128)} %bitcast.1.rank_ref, bf16[16,352,128]{2,1,0:T(8,128)(2,1)} %all-to-all-done.1.q_ref, bf16[6,4,192,256]{3,2,1,0:T(8,128)(2,1)} %regroup.1.near_ref), custom_call_target="tpu_custom_call" | custom-call | tf_op jit(solution)/shard_map/attend/pallas_call | solution.py:351
  114.1 5.0 %all-to-all-start.2 = ((bf16[16,6,48,128]{3,2,1,0:T(8,128)(2,1)}), bf16[16,6,48,128]{3,2,1,0:T(8,128)(2,1)S(1)}, u32[]{:S(2)}, u32[]{:S(2)}) async-start(bf16[16,6,48,128]{3,2,1,0:T(8,128)(2,1)} %attend.1), calls=%async_computation.2 | async-start | bytes 2359296 | tf_op jit(solution)/shard_map/all_to_all | solution.py:366
  119.1 0.0 copy-done
  119.1 1.1 constant_dynamic-slice_fusion
  120.2 2.0 %collective-permute-start.1 = (bf16[768,768]{1,0:T(8,128)(2,1)}, bf16[768,768]{1,0:T(8,128)(2,1)}, u32[]{:S(2)}, u32[]{:S(2)}) collective-permute-start(bf16[768,768]{1,0:T(8,128)(2,1)} %constant_dynamic-slice_fusion), channel_id=1, source_target_pairs={{0,1},{1,0},{2,3},{3,2},{4,5},{5,4},{6,7},{7,6},{8,9},{9,8},{10,11... | collective-permute-start | bytes 3538952 | tf_op jit(solution)/shard_map/ppermute | solution.py:281
  122.2 24.0 %all-to-all-done.2.back_ref = bf16[16,6,48,128]{3,2,1,0:T(8,128)(2,1)S(1)} async-done(((bf16[16,6,48,128]{3,2,1,0:T(8,128)(2,1)}), bf16[16,6,48,128]{3,2,1,0:T(8,128)(2,1)S(1)}, u32[]{:S(2)}, u32[]{:S(2)}) %all-to-all-start.2) | async-done | bytes 1179680 | tf_op jit(solution)/shard_map/all_to_all | solution.py:366
  146.3 0.0 copy-start.1
  146.3 0.9 copy-done.1
  147.2 3.0 %unpack.1 = bf16[384,768]{1,0:T(8,128)(2,1)} custom-call(s32[384,128]{1,0:T(8,128)S(1)} %copy-done.1, bf16[16,6,48,128]{3,2,1,0:T(8,128)(2,1)S(1)} %all-to-all-done.2.back_ref), custom_call_target="tpu_custom_call" | custom-call | tf_op jit(solution)/shard_map/unpack/pallas_call | solution.py:368
  150.2 2.5 %collective-permute-start = (bf16[384,768]{1,0:T(8,128)(2,1)}, bf16[384,768]{1,0:T(8,128)(2,1)S(1)}, u32[]{:S(2)}, u32[]{:S(2)}) collective-permute-start(bf16[384,768]{1,0:T(8,128)(2,1)} %unpack.1), channel_id=1, source_target_pairs={{0,1},{1,0},{2,3},{3,2},{4,5},{5,4},{6,7},{7,6},{8,9},{9,8},{10,11... | collective-permute-start | bytes 1769480 | tf_op jit(solution)/shard_map/ppermute | solution.py:377
  152.7 1.7 %fusion.1 = f32[384,768]{1,0:T(8,128)S(1)} fusion(bf16[384,768]{1,0:T(8,128)(2,1)} %unpack.1, bf16[768,1536]{1,0:T(8,128)(2,1)S(1)} %copy-done, s32[]{:T(128)S(6)} %select_n.6), kind=kOutput, calls=%fused_computation.2 | convolution fusion | flops 452984832 | bytes 2949124 | tf_op jit(solution)/shard_map/dot_general | solution.py:27
  154.4 0.0 collective-permute-done.1
  154.4 0.1 collective-permute-done
  154.5 2.7 %fusion = bf16[384,768]{1,0:T(8,128)(2,1)} fusion(f32[384,768]{1,0:T(8,128)S(1)} %fusion.1, bf16[384,768]{1,0:T(8,128)(2,1)S(1)} %collective-permute-done, bf16[768,768]{1,0:T(8,128)(2,1)} %collective-permute-done.1), kind=kOutput, calls=%fused_computation.1 | convolution fusion | flops 453574656 | bytes 3538944 | tf_op jit(solution)/shard_map/dot_general | solution.py:27
Async XLA Ops:
  0.0 119.1 %copy-start = (bf16[768,1536]{1,0:T(8,128)(2,1)S(1)}, bf16[768,1536]{1,0:T(8,128)(2,1)}, u32[]{:S(2)}) copy-start(bf16[768,1536]{1,0:T(8,128)(2,1)} %param.9) | copy-start | bytes 7077892
  5.4 58.0 %all-to-all-start = ((bf16[16,6,48,256]{3,2,1,0:T(8,128)(2,1)}), bf16[16,6,48,256]{3,2,1,0:T(8,128)(2,1)}, u32[]{:S(2)}, u32[]{:S(2)}) async-start(bf16[16,6,48,256]{3,2,1,0:T(8,128)(2,1)} %get-tuple-element.11), calls=%async_computation | async-start | bytes 4718592 | tf_op jit(solution)/shard_map/all_to_all | solution.py:303
  67.0 39.7 %all-to-all-start.1 = ((bf16[16,352,128]{2,1,0:T(8,128)(2,1)}), bf16[16,352,128]{2,1,0:T(8,128)(2,1)}, u32[]{:S(2)}, u32[]{:S(2)}) async-start(bf16[16,352,128]{2,1,0:T(8,128)(2,1)} %centers.1), calls=%async_computation.1 | async-start | bytes 2883584 | tf_op jit(solution)/shard_map/all_to_all | solution.py:334
  114.1 32.2 %all-to-all-start.2 = ((bf16[16,6,48,128]{3,2,1,0:T(8,128)(2,1)}), bf16[16,6,48,128]{3,2,1,0:T(8,128)(2,1)S(1)}, u32[]{:S(2)}, u32[]{:S(2)}) async-start(bf16[16,6,48,128]{3,2,1,0:T(8,128)(2,1)} %attend.1), calls=%async_computation.2 | async-start | bytes 2359296 | tf_op jit(solution)/shard_map/all_to_all | solution.py:366
  120.2 34.2 %collective-permute-start.1 = (bf16[768,768]{1,0:T(8,128)(2,1)}, bf16[768,768]{1,0:T(8,128)(2,1)}, u32[]{:S(2)}, u32[]{:S(2)}) collective-permute-start(bf16[768,768]{1,0:T(8,128)(2,1)} %constant_dynamic-slice_fusion), channel_id=1, source_target_pairs={{0,1},{1,0},{2,3},{3,2},{4,5},{5,4},{6,7},{7,6},{8,9},{9,8},{10,11... | collective-permute-start | bytes 3538952 | tf_op jit(solution)/shard_map/ppermute | solution.py:281
  146.3 0.9 copy-start.1
  150.2 4.4 %collective-permute-start = (bf16[384,768]{1,0:T(8,128)(2,1)}, bf16[384,768]{1,0:T(8,128)(2,1)S(1)}, u32[]{:S(2)}, u32[]{:S(2)}) collective-permute-start(bf16[384,768]{1,0:T(8,128)(2,1)} %unpack.1), channel_id=1, source_target_pairs={{0,1},{1,0},{2,3},{3,2},{4,5},{5,4},{6,7},{7,6},{8,9},{9,8},{10,11... | collective-permute-start | bytes 1769480 | tf_op jit(solution)/shard_map/ppermute | solution.py:377

commit v4 on v3

--- a/solution.py
+++ b/solution.py
@@ -100,9 +100,14 @@
         pair_ref[0, e] = nn_dot(perm_ref[e], pairs).astype(BF16)
 
 
-def centers_kernel(cap, recv_ref, buffer_ref, send_ref, block_ref, sem):
+def centers_kernel(cap, recv_hbm, buffer_ref, send_ref, recv_ref, block_ref, in_sem, sem):
     del buffer_ref
     n_seq, heads, rows, _ = recv_ref.shape
+    incoming = [
+        pltpu.make_async_copy(recv_hbm.at[:, h], recv_ref.at[:, h], in_sem.at[h]) for h in range(heads)
+    ]
+    for copy in incoming:
+        copy.start()
     _, extra, hd = block_ref.shape
     owned = heads * CL_DEV
     row = iota((rows, 1), 0)
@@ -110,6 +115,7 @@
     total = jnp.zeros((extra, hd), F32)
     count = jnp.zeros((extra, 1), F32)
     for h in range(heads):
+        incoming[h].wait()
         key = recv_ref[:, h, :, :hd].astype(F32)
         value = jnp.sum(recv_ref[:, h, :, hd:].astype(F32), axis=0)
         empty = key > 0.5 * EMPTY
@@ -244,9 +250,19 @@
         place = jnp.sum(
             jnp.where(iota((tok, 128), 1) == h + i, column, 0), axis=1, keepdims=True
         )
-        hot = one_zero(iota((tok, slots), 1) == place)
+        lane = lax.broadcasted_iota(jnp.int16, (tok, slots), 1)
+        hot = jnp.where(lane == place.astype(jnp.int16), jnp.ones(lane.shape, BF16), jnp.zeros(lane.shape, BF16))
         answer = nn_dot(hot, back_ref[:, i].reshape(slots, hd))
         out_ref[:, i * hd : (i + 1) * hd] = answer.astype(BF16)
+
+
+def own_part_kernel(attended_ref, mine_ref, other_ref, part_ref, staged_ref):
+    part_ref[...] = nn_dot(attended_ref[...], mine_ref[...])
+    staged_ref[...] = other_ref[...]
+
+
+def finish_kernel(part_ref, partner_ref, weight_ref, out_ref):
+    out_ref[...] = (part_ref[...] + nn_dot(partner_ref[...], weight_ref[...])).astype(BF16)
 
 
 def per_device(queries, keys, values, membership, w_out):
@@ -265,7 +281,7 @@
     per_step = 2
     params = pltpu.CompilerParams(
         dimension_semantics=("arbitrary",),
-        vmem_limit_bytes=60 * 1024 * 1024,
+        vmem_limit_bytes=63 * 1024 * 1024,
     )
     small = pltpu.CompilerParams(
         dimension_semantics=("arbitrary",),
@@ -290,6 +306,9 @@
     def slot_array(depth):
         return jax.ShapeDtypeStruct((n_seq, heads, rows, depth), BF16)
 
+    anywhere = pl.BlockSpec(memory_space=pl.ANY)
+    in_vmem = pl.BlockSpec(memory_space=pltpu.VMEM)
+    whole_params = pltpu.CompilerParams(vmem_limit_bytes=params.vmem_limit_bytes)
     send_kv, place = pl.pallas_call(
         functools.partial(pack_kv_kernel, rows, cap),
         grid=(heads // per_step,),
@@ -316,19 +335,19 @@
         name="pack_q",
     )(place, queries)
 
-    anywhere = pl.BlockSpec(memory_space=pl.ANY)
-    in_vmem = pl.BlockSpec(memory_space=pltpu.VMEM)
     send_q = pl.pallas_call(
         functools.partial(centers_kernel, cap),
-        in_specs=[in_vmem, anywhere],
+        in_specs=[anywhere, anywhere],
         out_specs=anywhere,
         out_shape=q_array,
         scratch_shapes=[
+            pltpu.VMEM((n_seq, heads, rows, 2 * hd), BF16),
             pltpu.VMEM((n_seq, extra, hd), BF16),
+            pltpu.SemaphoreType.DMA((heads,)),
             pltpu.SemaphoreType.DMA,
         ],
         input_output_aliases={1: 0},
-        compiler_params=pltpu.CompilerParams(vmem_limit_bytes=params.vmem_limit_bytes),
+        compiler_params=whole_params,
         name="centers",
     )(received_kv, send_q)
     received_q = exchange(send_q)
@@ -367,16 +386,34 @@
 
     attended = pl.pallas_call(
         unpack_kernel,
-        grid=(heads // per_step,),
-        in_specs=[column, slot_block(hd, per_step)],
-        out_specs=matrix,
+        grid=(heads // many,),
+        in_specs=[column, slot_block(hd, many)],
+        out_specs=pl.BlockSpec((tok, many * hd), lambda h: (0, h)),
         out_shape=jax.ShapeDtypeStruct((tok, heads * hd), BF16),
         compiler_params=small,
         name="unpack",
     )(columns, returned)
     partner = lax.ppermute(attended, "head", swap)
-    result = nn_dot(attended, mine) + nn_dot(partner, other)
-    return result.astype(BF16)
+    tail = pltpu.CompilerParams(vmem_limit_bytes=16 * 1024 * 1024)
+    own_part, staged = pl.pallas_call(
+        own_part_kernel,
+        in_specs=[in_vmem] * 3,
+        out_specs=[in_vmem] * 2,
+        out_shape=[
+            jax.ShapeDtypeStruct((tok, width), F32),
+            jax.ShapeDtypeStruct(other.shape, BF16),
+        ],
+        compiler_params=tail,
+        name="own_part",
+    )(attended, mine, other)
+    return pl.pallas_call(
+        finish_kernel,
+        in_specs=[in_vmem] * 3,
+        out_specs=in_vmem,
+        out_shape=jax.ShapeDtypeStruct((tok, width), BF16),
+        compiler_params=tail,
+        name="finish",
+    )(own_part, partner, staged)
 
 
 def solution(mesh):

time: 158 us -> 154 us (0.975)
  matrix products: 4.4 us -> 0 us
  local copies, waits for them, and re-layouts: 2.04 us -> 3.72 us
    dot_general x2 -> x0, matrix products: 4.4 us -> none  [nn_dot(): return jnp.dot(a, b, preferred_element_type=F32)]
    dynamic_slice x1, local copies, waits for them, and re-layouts: 1.1 us -> 2.8 us  [per_device(): other = lax.dynamic_slice_in_dim(w_out, (1 - group) * width, width, 1)]
    all_to_all x1, waiting for transfers between devices: 24 us -> 22.4 us  [per_device(): returned = exchange(answers)]
    pallas_call x2 -> x4, Pallas kernels: 6.49 us -> 6.5 us  [the longest x1 2.74 us: per_device(): pl.pallas_call(functools.partial(centers_kernel, cap), in_specs=[anywhere...]
where the time goes in v4:
time: 154 us
  waiting for transfers between devices  97.6 us (63%)
  Pallas kernels  29.3 us (19%)
  starting transfers between devices  23 us (15%)
  local copies, waits for them, and re-layouts  3.72 us (2%)
    all_to_all x1, waiting for transfers between devices, per_device(): received_kv = exchange(send_kv)  47.5 us
    all_to_all x1, waiting for transfers between devices, per_device(): received_q = exchange(send_q)  26.7 us
    all_to_all x1, waiting for transfers between devices, per_device(): returned = exchange(answers)  22.4 us
    pallas_call x1, Pallas kernels, per_device(): pl.pallas_call(functools.partial(attend_kernel, cap), grid=(heads // many...  7.37 us
    all_to_all x1, starting transfers between devices, per_device(): received_kv = exchange(send_kv)  6.67 us
    all_to_all x1, starting transfers between devices, per_device(): received_q = exchange(send_q)  6.62 us
    pallas_call x1, Pallas kernels, per_device(): pl.pallas_call(functools.partial(regroup_kernel, rows, cap), grid=(heads,...  6.36 us
    pallas_call x1, Pallas kernels, per_device(): pl.pallas_call(functools.partial(pack_kv_kernel, rows, cap), grid=(heads...  5.25 us
  transfers between devices with their start and end apart: 5, of which 4 were waited for; matrix products, arithmetic and copies ran while one was open for 2% of the time, Pallas kernels for 8%

profile of v4, /device:TPU:9, one launch (start us, length us, event | category | flops | bytes accessed | tf_op | source)
XLA Modules:
  0.0 153.6 jit_solution(12557083692783636424)
XLA Ops:
  0.0 5.2 %pack_kv.1 = (bf16[16,6,48,256]{3,2,1,0:T(8,128)(2,1)}, s32[6,1,384]{2,1,0:T(1,128)}) custom-call(s32[6,1,384]{2,1,0:T(1,128)} %bitcast.2, bf16[384,768]{1,0:T(8,128)(2,1)} %k_ref.1, bf16[384,768]{1,0:T(8,128)(2,1)} %v_ref.1), custom_call_target="tpu_custom_call" | custom-call | tf_op jit(solution)/shard_map/pack_kv/pallas_call | solution.py:312
  5.2 6.7 %all-to-all-start = ((bf16[16,6,48,256]{3,2,1,0:T(8,128)(2,1)}), bf16[16,6,48,256]{3,2,1,0:T(8,128)(2,1)}, u32[]{:S(2)}, u32[]{:S(2)}) async-start(bf16[16,6,48,256]{3,2,1,0:T(8,128)(2,1)} %get-tuple-element.13), calls=%async_computation | async-start | bytes 4718592 | tf_op jit(solution)/shard_map/all_to_all | solution.py:322
  11.9 3.8 %pack_q.1 = (bf16[16,352,128]{2,1,0:T(8,128)(2,1)}, s32[384,128]{1,0:T(8,128)}) custom-call(s32[6,1,384]{2,1,0:T(1,128)} %get-tuple-element.11.place_ref, bf16[384,768]{1,0:T(8,128)(2,1)} %q_ref.1), custom_call_target="tpu_custom_call" | custom-call | tf_op jit(solution)/shard_map/pack_q/pallas_call | solution.py:328
  15.7 47.5 %all-to-all-done.recv_hbm.recv_ref = bf16[16,6,48,256]{3,2,1,0:T(8,128)(2,1)} async-done(((bf16[16,6,48,256]{3,2,1,0:T(8,128)(2,1)}), bf16[16,6,48,256]{3,2,1,0:T(8,128)(2,1)}, u32[]{:S(2)}, u32[]{:S(2)}) %all-to-all-start) | async-done | bytes 2359328 | tf_op jit(solution)/shard_map/all_to_all | solution.py:322
  63.3 2.7 %centers.1 = bf16[16,352,128]{2,1,0:T(8,128)(2,1)} custom-call(bf16[16,6,48,256]{3,2,1,0:T(8,128)(2,1)} %all-to-all-done.recv_hbm.recv_ref, bf16[16,352,128]{2,1,0:T(8,128)(2,1)} %get-tuple-element.14.buffer_ref), custom_call_target="tpu_custom_call", output_to_operand_aliasing={{}: (1, {})} | custom-call | tf_op jit(solution)/shard_map/centers/pallas_call | solution.py:338
  66.0 6.6 %all-to-all-start.1 = ((bf16[16,352,128]{2,1,0:T(8,128)(2,1)}), bf16[16,352,128]{2,1,0:T(8,128)(2,1)}, u32[]{:S(2)}, u32[]{:S(2)}) async-start(bf16[16,352,128]{2,1,0:T(8,128)(2,1)} %centers.1), calls=%async_computation.1 | async-start | bytes 2883584 | tf_op jit(solution)/shard_map/all_to_all | solution.py:353
  72.6 6.4 %regroup.1.near_ref = bf16[6,4,192,256]{3,2,1,0:T(8,128)(2,1)} custom-call(bf16[16,6,48,256]{3,2,1,0:T(8,128)(2,1)} %all-to-all-done.recv_hbm.recv_ref), custom_call_target="tpu_custom_call" | custom-call | tf_op jit(solution)/shard_map/regroup/pallas_call | solution.py:358
  79.0 26.7 %all-to-all-done.1.q_ref = bf16[16,352,128]{2,1,0:T(8,128)(2,1)} async-done(((bf16[16,352,128]{2,1,0:T(8,128)(2,1)}), bf16[16,352,128]{2,1,0:T(8,128)(2,1)}, u32[]{:S(2)}, u32[]{:S(2)}) %all-to-all-start.1) | async-done | bytes 1441824 | tf_op jit(solution)/shard_map/all_to_all | solution.py:353
  105.7 7.4 %attend.1 = bf16[16,6,48,128]{3,2,1,0:T(8,128)(2,1)} custom-call(s32[1]{0:T(128)} %bitcast.1.rank_ref, bf16[16,352,128]{2,1,0:T(8,128)(2,1)} %all-to-all-done.1.q_ref, bf16[6,4,192,256]{3,2,1,0:T(8,128)(2,1)} %regroup.1.near_ref), custom_call_target="tpu_custom_call" | custom-call | tf_op jit(solution)/shard_map/attend/pallas_call | solution.py:370
  113.1 5.0 %all-to-all-start.2 = ((bf16[16,6,48,128]{3,2,1,0:T(8,128)(2,1)}), bf16[16,6,48,128]{3,2,1,0:T(8,128)(2,1)S(1)}, u32[]{:S(2)}, u32[]{:S(2)}) async-start(bf16[16,6,48,128]{3,2,1,0:T(8,128)(2,1)} %attend.1), calls=%async_computation.2 | async-start | bytes 2359296 | tf_op jit(solution)/shard_map/all_to_all | solution.py:385
  118.1 2.8 %constant_dynamic-slice_fusion = (bf16[768,768]{1,0:T(8,128)(2,1)}, bf16[768,768]{1,0:T(8,128)(2,1)S(1)}) fusion(bf16[768,1536]{1,0:T(8,128)(2,1)} %param.9, s32[]{:T(128)S(6)} %select_n.7, s32[]{:T(128)S(6)} %select_n.6), kind=kLoop, calls=%fused_computation | loop fusion | bytes 4718600 | tf_op jit(solution)/shard_map/dynamic_slice | solution.py:296
  120.9 2.0 %collective-permute-start = (bf16[768,768]{1,0:T(8,128)(2,1)}, bf16[768,768]{1,0:T(8,128)(2,1)S(1)}, u32[]{:S(2)}, u32[]{:S(2)}) collective-permute-start(bf16[768,768]{1,0:T(8,128)(2,1)} %get-tuple-element.17), channel_id=1, source_target_pairs={{0,1},{1,0},{2,3},{3,2},{4,5},{5,4},{6,7},{7,6},{8,9},{9,8},{10,11... | collective-permute-start | bytes 3538952 | tf_op jit(solution)/shard_map/ppermute | solution.py:297
  123.0 22.4 %all-to-all-done.2.back_ref = bf16[16,6,48,128]{3,2,1,0:T(8,128)(2,1)S(1)} async-done(((bf16[16,6,48,128]{3,2,1,0:T(8,128)(2,1)}), bf16[16,6,48,128]{3,2,1,0:T(8,128)(2,1)S(1)}, u32[]{:S(2)}, u32[]{:S(2)}) %all-to-all-start.2) | async-done | bytes 1179680 | tf_op jit(solution)/shard_map/all_to_all | solution.py:385
  145.3 0.0 copy-start
  145.3 0.9 copy-done
  146.2 1.7 %unpack.1.attended_ref = bf16[384,768]{1,0:T(8,128)(2,1)S(1)} custom-call(s32[384,128]{1,0:T(8,128)S(1)} %copy-done, bf16[16,6,48,128]{3,2,1,0:T(8,128)(2,1)S(1)} %all-to-all-done.2.back_ref), custom_call_target="tpu_custom_call" | custom-call | tf_op jit(solution)/shard_map/unpack/pallas_call | solution.py:387
  147.9 2.6 %collective-permute-start.1 = (bf16[384,768]{1,0:T(8,128)(2,1)S(1)}, bf16[384,768]{1,0:T(8,128)(2,1)S(1)}, u32[]{:S(2)}, u32[]{:S(2)}) collective-permute-start(bf16[384,768]{1,0:T(8,128)(2,1)S(1)} %unpack.1.attended_ref), channel_id=1, source_target_pairs={{0,1},{1,0},{2,3},{3,2},{4,5},{5,4},{6,7},{7,6},{8,9},{9,8},{10,11... | collective-permute-start | bytes 1769480 | tf_op jit(solution)/shard_map/ppermute | solution.py:396
  150.5 0.0 collective-permute-done.other_ref
  150.5 0.7 own_part.1
  151.2 1.0 collective-permute-done.1.partner_ref
  152.2 1.4 finish.1
Async XLA Ops:
  5.2 58.0 %all-to-all-start = ((bf16[16,6,48,256]{3,2,1,0:T(8,128)(2,1)}), bf16[16,6,48,256]{3,2,1,0:T(8,128)(2,1)}, u32[]{:S(2)}, u32[]{:S(2)}) async-start(bf16[16,6,48,256]{3,2,1,0:T(8,128)(2,1)} %get-tuple-element.13), calls=%async_computation | async-start | bytes 4718592 | tf_op jit(solution)/shard_map/all_to_all | solution.py:322
  66.0 39.7 %all-to-all-start.1 = ((bf16[16,352,128]{2,1,0:T(8,128)(2,1)}), bf16[16,352,128]{2,1,0:T(8,128)(2,1)}, u32[]{:S(2)}, u32[]{:S(2)}) async-start(bf16[16,352,128]{2,1,0:T(8,128)(2,1)} %centers.1), calls=%async_computation.1 | async-start | bytes 2883584 | tf_op jit(solution)/shard_map/all_to_all | solution.py:353
  113.1 32.2 %all-to-all-start.2 = ((bf16[16,6,48,128]{3,2,1,0:T(8,128)(2,1)}), bf16[16,6,48,128]{3,2,1,0:T(8,128)(2,1)S(1)}, u32[]{:S(2)}, u32[]{:S(2)}) async-start(bf16[16,6,48,128]{3,2,1,0:T(8,128)(2,1)} %attend.1), calls=%async_computation.2 | async-start | bytes 2359296 | tf_op jit(solution)/shard_map/all_to_all | solution.py:385
  120.9 29.6 %collective-permute-start = (bf16[768,768]{1,0:T(8,128)(2,1)}, bf16[768,768]{1,0:T(8,128)(2,1)S(1)}, u32[]{:S(2)}, u32[]{:S(2)}) collective-permute-start(bf16[768,768]{1,0:T(8,128)(2,1)} %get-tuple-element.17), channel_id=1, source_target_pairs={{0,1},{1,0},{2,3},{3,2},{4,5},{5,4},{6,7},{7,6},{8,9},{9,8},{10,11... | collective-permute-start | bytes 3538952 | tf_op jit(solution)/shard_map/ppermute | solution.py:297
  145.3 0.9 copy-start
  147.9 4.2 %collective-permute-start.1 = (bf16[384,768]{1,0:T(8,128)(2,1)S(1)}, bf16[384,768]{1,0:T(8,128)(2,1)S(1)}, u32[]{:S(2)}, u32[]{:S(2)}) collective-permute-start(bf16[384,768]{1,0:T(8,128)(2,1)S(1)} %unpack.1.attended_ref), channel_id=1, source_target_pairs={{0,1},{1,0},{2,3},{3,2},{4,5},{5,4},{6,7},{7,6},{8,9},{9,8},{10,11... | collective-permute-start | bytes 1769480 | tf_op jit(solution)/shard_map/ppermute | solution.py:396

commit v5 on v4

--- a/solution.py
+++ b/solution.py
@@ -185,43 +185,54 @@
 
 
 def attend_kernel(
-    cap, rank_ref, q_ref, near_ref, out_ref,
-    far_key_ref, far_value_ref, mask_ref, side_ref,
+    cap, rank_ref, q_hbm, near_hbm, out_hbm, far_key_ref, far_value_ref, mask_ref, side_ref,
+    q_ref, near_ref, out_ref, q_sem, in_sem, out_sem,
 ):
-    step = pl.program_id(0)
-    n_seq, per_step, rows, hd = out_ref.shape
-    heads = far_key_ref.shape[0]
+    n_seq, heads, rows, hd = out_ref.shape
     group = n_seq * 16
     tiles = [tile_clusters(tile, rows, cap) for tile in range(rows // 16)]
-
-    @pl.when(step == 0)
-    def _():
-        lane = iota((group, hd), 1)
-        row = lax.rem(iota((group, hd), 0), 16)
-        for tile, clusters in enumerate(tiles):
-            place = row + tile * 16
-            for j, e in enumerate(clusters):
-                inside = place >= e * cap
-                if e + 1 < CL_DEV:
-                    inside = inside & (place < (e + 1) * cap)
-                mask_ref[tile, j] = one_zero(inside)
-                side_ref[tile, j] = one_zero(inside & ((lane < 3) | (lane == 3 + e)))
-        prepare_far(rank_ref[0], q_ref[:, heads * rows :], heads, far_key_ref, far_value_ref)
+    incoming, outgoing = [], []
+    for h in range(heads):
+        incoming.append(pltpu.make_async_copy(near_hbm.at[h], near_ref.at[h], in_sem.at[h]))
+        outgoing.append(pltpu.make_async_copy(out_ref.at[:, h], out_hbm.at[:, h], out_sem.at[h]))
+    split = heads * rows
+    means, slots = pl.ds(split, q_ref.shape[1] - split), pl.ds(0, split)
+    means = pltpu.make_async_copy(q_hbm.at[:, means], q_ref.at[:, means], q_sem.at[0])
+    slots = pltpu.make_async_copy(q_hbm.at[:, slots], q_ref.at[:, slots], q_sem.at[1])
+    means.start()
+    slots.start()
+    for copy in incoming:
+        copy.start()
+
+    lane = iota((group, hd), 1)
+    row = lax.rem(iota((group, hd), 0), 16)
+    for tile, clusters in enumerate(tiles):
+        place = row + tile * 16
+        for j, e in enumerate(clusters):
+            inside = place >= e * cap
+            if e + 1 < CL_DEV:
+                inside = inside & (place < (e + 1) * cap)
+            mask_ref[tile, j] = one_zero(inside)
+            side_ref[tile, j] = one_zero(inside & ((lane < 3) | (lane == 3 + e)))
+    means.wait()
+    prepare_far(rank_ref[0], q_ref[:, heads * rows :], heads, far_key_ref, far_value_ref)
+    slots.wait()
+    for copy in incoming:
+        copy.wait()
 
     scale = math.log2(math.e) / math.sqrt(hd)
-    for i in range(per_step):
-        h = step * per_step + i
+    for h in range(heads):
         far_key, far_value = far_key_ref[h], far_value_ref[h]
         keys, values = [], []
         for e in range(CL_DEV):
-            key, value = near_ref[i, e, :, :hd], near_ref[i, e, :, hd:]
+            key, value = near_ref[h, e, :, :hd], near_ref[h, e, :, hd:]
             side = jnp.where(key > 0.5 * EMPTY, NEG, 0.0).astype(BF16)
             keys.append(jnp.concatenate([jnp.concatenate([key, side], 1), far_key], 0))
             ones = jnp.ones(value.shape, BF16)
             values.append(jnp.concatenate([jnp.concatenate([value, ones], 1), far_value], 0))
         for tile, clusters in enumerate(tiles):
-            start = pl.multiple_of(h * rows + tile * 16, 16)
-            query = q_ref[:, pl.ds(start, 16)].reshape(group, hd)
+            start = h * rows + tile * 16
+            query = q_ref[:, start : start + 16].reshape(group, hd)
             wide = []
             for j in range(len(clusters)):
                 wide += [query * mask_ref[tile, j], side_ref[tile, j]]
@@ -237,7 +248,10 @@
             inverse = pl.reciprocal(total, approx=True)
             inverse = inverse * (2.0 - total * inverse)
             answer = (mixed[:, :hd] * inverse).astype(BF16)
-            out_ref[:, i, tile * 16 : tile * 16 + 16] = answer.reshape(n_seq, 16, hd)
+            out_ref[:, h, tile * 16 : tile * 16 + 16] = answer.reshape(n_seq, 16, hd)
+        outgoing[h].start()
+    for copy in outgoing:
+        copy.wait()
 
 
 def unpack_kernel(column_ref, back_ref, out_ref):
@@ -366,24 +380,29 @@
         name="regroup",
     )(received_kv)
 
-    many = 3
     answers = pl.pallas_call(
         functools.partial(attend_kernel, cap),
-        grid=(heads // many,),
-        in_specs=[pl.BlockSpec(memory_space=pltpu.SMEM), in_vmem, near_block(many)],
-        out_specs=slot_block(hd, many),
+        in_specs=[pl.BlockSpec(memory_space=pltpu.SMEM), anywhere, anywhere],
+        out_specs=anywhere,
         out_shape=slot_array(hd),
         scratch_shapes=[
             pltpu.VMEM((heads, clusters, 2 * hd), BF16),
             pltpu.VMEM((heads, clusters, 2 * hd), BF16),
             pltpu.VMEM((rows // 16, CL_DEV, n_seq * 16, hd), BF16),
             pltpu.VMEM((rows // 16, CL_DEV, n_seq * 16, hd), BF16),
+            pltpu.VMEM((n_seq, all_rows, hd), BF16),
+            pltpu.VMEM((heads, CL_DEV, near, 2 * hd), BF16),
+            pltpu.VMEM((n_seq, heads, rows, hd), BF16),
+            pltpu.SemaphoreType.DMA((2,)),
+            pltpu.SemaphoreType.DMA((heads,)),
+            pltpu.SemaphoreType.DMA((heads,)),
         ],
-        compiler_params=params,
+        compiler_params=whole_params,
         name="attend",
     )(rank.reshape(1), received_q, near_pairs)
     returned = exchange(answers)
 
+    many = 3
     attended = pl.pallas_call(
         unpack_kernel,
         grid=(heads // many,),

time: 154 us -> 154 us (level)
  no operation moved by 1% of the time
where the time goes in v5:
time: 154 us; the launch traced here: 153 us
  waiting for transfers between devices  97.6 us (63%)
  Pallas kernels  28.7 us (19%)
  starting transfers between devices  23 us (15%)
  local copies, waits for them, and re-layouts  3.72 us (2%)
    all_to_all x1, waiting for transfers between devices, per_device(): received_kv = exchange(send_kv)  47.5 us
    all_to_all x1, waiting for transfers between devices, per_device(): received_q = exchange(send_q)  26.7 us
    all_to_all x1, waiting for transfers between devices, per_device(): returned = exchange(answers)  22.3 us
    pallas_call x1, Pallas kernels, per_device(): pl.pallas_call(functools.partial(attend_kernel, cap), in_specs=[pl.BlockS...  6.83 us
    all_to_all x1, starting transfers between devices, per_device(): received_kv = exchange(send_kv)  6.67 us
    all_to_all x1, starting transfers between devices, per_device(): received_q = exchange(send_q)  6.62 us
    pallas_call x1, Pallas kernels, per_device(): pl.pallas_call(functools.partial(regroup_kernel, rows, cap), grid=(heads,...  6.36 us
    pallas_call x1, Pallas kernels, per_device(): pl.pallas_call(functools.partial(pack_kv_kernel, rows, cap), grid=(heads...  5.25 us
  transfers between devices with their start and end apart: 5, of which 4 were waited for; matrix products, arithmetic and copies ran while one was open for 2% of the time, Pallas kernels for 8%

profile of v5, /device:TPU:9, one launch (start us, length us, event | category | flops | bytes accessed | tf_op | source)
XLA Modules:
  0.0 153.1 jit_solution(1870038171716677457)
XLA Ops:
  0.0 5.2 %pack_kv.1 = (bf16[16,6,48,256]{3,2,1,0:T(8,128)(2,1)}, s32[6,1,384]{2,1,0:T(1,128)}) custom-call(s32[6,1,384]{2,1,0:T(1,128)} %bitcast.2, bf16[384,768]{1,0:T(8,128)(2,1)} %k_ref.1, bf16[384,768]{1,0:T(8,128)(2,1)} %v_ref.1), custom_call_target="tpu_custom_call" | custom-call | tf_op jit(solution)/shard_map/pack_kv/pallas_call | solution.py:326
  5.2 6.7 %all-to-all-start = ((bf16[16,6,48,256]{3,2,1,0:T(8,128)(2,1)}), bf16[16,6,48,256]{3,2,1,0:T(8,128)(2,1)}, u32[]{:S(2)}, u32[]{:S(2)}) async-start(bf16[16,6,48,256]{3,2,1,0:T(8,128)(2,1)} %get-tuple-element.13), calls=%async_computation | async-start | bytes 4718592 | tf_op jit(solution)/shard_map/all_to_all | solution.py:336
  11.9 3.8 %pack_q.1 = (bf16[16,352,128]{2,1,0:T(8,128)(2,1)}, s32[384,128]{1,0:T(8,128)}) custom-call(s32[6,1,384]{2,1,0:T(1,128)} %get-tuple-element.11.place_ref, bf16[384,768]{1,0:T(8,128)(2,1)} %q_ref.1), custom_call_target="tpu_custom_call" | custom-call | tf_op jit(solution)/shard_map/pack_q/pallas_call | solution.py:342
  15.7 47.5 %all-to-all-done.recv_hbm.recv_ref = bf16[16,6,48,256]{3,2,1,0:T(8,128)(2,1)} async-done(((bf16[16,6,48,256]{3,2,1,0:T(8,128)(2,1)}), bf16[16,6,48,256]{3,2,1,0:T(8,128)(2,1)}, u32[]{:S(2)}, u32[]{:S(2)}) %all-to-all-start) | async-done | bytes 2359328 | tf_op jit(solution)/shard_map/all_to_all | solution.py:336
  63.3 2.7 %centers.1 = bf16[16,352,128]{2,1,0:T(8,128)(2,1)} custom-call(bf16[16,6,48,256]{3,2,1,0:T(8,128)(2,1)} %all-to-all-done.recv_hbm.recv_ref, bf16[16,352,128]{2,1,0:T(8,128)(2,1)} %get-tuple-element.14.buffer_ref), custom_call_target="tpu_custom_call", output_to_operand_aliasing={{}: (1, {})} | custom-call | tf_op jit(solution)/shard_map/centers/pallas_call | solution.py:352
  66.0 6.6 %all-to-all-start.1 = ((bf16[16,352,128]{2,1,0:T(8,128)(2,1)}), bf16[16,352,128]{2,1,0:T(8,128)(2,1)}, u32[]{:S(2)}, u32[]{:S(2)}) async-start(bf16[16,352,128]{2,1,0:T(8,128)(2,1)} %centers.1), calls=%async_computation.1 | async-start | bytes 2883584 | tf_op jit(solution)/shard_map/all_to_all | solution.py:367
  72.6 6.4 %regroup.1.near_hbm = bf16[6,4,192,256]{3,2,1,0:T(8,128)(2,1)} custom-call(bf16[16,6,48,256]{3,2,1,0:T(8,128)(2,1)} %all-to-all-done.recv_hbm.recv_ref), custom_call_target="tpu_custom_call" | custom-call | tf_op jit(solution)/shard_map/regroup/pallas_call | solution.py:372
  79.0 26.7 %all-to-all-done.1.q_hbm = bf16[16,352,128]{2,1,0:T(8,128)(2,1)} async-done(((bf16[16,352,128]{2,1,0:T(8,128)(2,1)}), bf16[16,352,128]{2,1,0:T(8,128)(2,1)}, u32[]{:S(2)}, u32[]{:S(2)}) %all-to-all-start.1) | async-done | bytes 1441824 | tf_op jit(solution)/shard_map/all_to_all | solution.py:367
  105.7 6.8 %attend.1 = bf16[16,6,48,128]{3,2,1,0:T(8,128)(2,1)} custom-call(s32[1]{0:T(128)} %bitcast.1.rank_ref, bf16[16,352,128]{2,1,0:T(8,128)(2,1)} %all-to-all-done.1.q_hbm, bf16[6,4,192,256]{3,2,1,0:T(8,128)(2,1)} %regroup.1.near_hbm), custom_call_target="tpu_custom_call" | custom-call | tf_op jit(solution)/shard_map/attend/pallas_call | solution.py:383
  112.6 5.0 %all-to-all-start.2 = ((bf16[16,6,48,128]{3,2,1,0:T(8,128)(2,1)}), bf16[16,6,48,128]{3,2,1,0:T(8,128)(2,1)S(1)}, u32[]{:S(2)}, u32[]{:S(2)}) async-start(bf16[16,6,48,128]{3,2,1,0:T(8,128)(2,1)} %attend.1), calls=%async_computation.2 | async-start | bytes 2359296 | tf_op jit(solution)/shard_map/all_to_all | solution.py:403
  117.6 2.8 %constant_dynamic-slice_fusion = (bf16[768,768]{1,0:T(8,128)(2,1)}, bf16[768,768]{1,0:T(8,128)(2,1)S(1)}) fusion(bf16[768,1536]{1,0:T(8,128)(2,1)} %param.9, s32[]{:T(128)S(6)} %select_n.7, s32[]{:T(128)S(6)} %select_n.6), kind=kLoop, calls=%fused_computation | loop fusion | bytes 4718600 | tf_op jit(solution)/shard_map/dynamic_slice | solution.py:310
  120.4 2.0 %collective-permute-start = (bf16[768,768]{1,0:T(8,128)(2,1)}, bf16[768,768]{1,0:T(8,128)(2,1)S(1)}, u32[]{:S(2)}, u32[]{:S(2)}) collective-permute-start(bf16[768,768]{1,0:T(8,128)(2,1)} %get-tuple-element.17), channel_id=1, source_target_pairs={{0,1},{1,0},{2,3},{3,2},{4,5},{5,4},{6,7},{7,6},{8,9},{9,8},{10,11... | collective-permute-start | bytes 3538952 | tf_op jit(solution)/shard_map/ppermute | solution.py:311
  122.4 22.3 %all-to-all-done.2.back_ref = bf16[16,6,48,128]{3,2,1,0:T(8,128)(2,1)S(1)} async-done(((bf16[16,6,48,128]{3,2,1,0:T(8,128)(2,1)}), bf16[16,6,48,128]{3,2,1,0:T(8,128)(2,1)S(1)}, u32[]{:S(2)}, u32[]{:S(2)}) %all-to-all-start.2) | async-done | bytes 1179680 | tf_op jit(solution)/shard_map/all_to_all | solution.py:403
  144.8 0.0 copy-start
  144.8 0.9 copy-done
  145.7 1.7 %unpack.1.attended_ref = bf16[384,768]{1,0:T(8,128)(2,1)S(1)} custom-call(s32[384,128]{1,0:T(8,128)S(1)} %copy-done, bf16[16,6,48,128]{3,2,1,0:T(8,128)(2,1)S(1)} %all-to-all-done.2.back_ref), custom_call_target="tpu_custom_call" | custom-call | tf_op jit(solution)/shard_map/unpack/pallas_call | solution.py:406
  147.4 2.6 %collective-permute-start.1 = (bf16[384,768]{1,0:T(8,128)(2,1)S(1)}, bf16[384,768]{1,0:T(8,128)(2,1)S(1)}, u32[]{:S(2)}, u32[]{:S(2)}) collective-permute-start(bf16[384,768]{1,0:T(8,128)(2,1)S(1)} %unpack.1.attended_ref), channel_id=1, source_target_pairs={{0,1},{1,0},{2,3},{3,2},{4,5},{5,4},{6,7},{7,6},{8,9},{9,8},{10,11... | collective-permute-start | bytes 1769480 | tf_op jit(solution)/shard_map/ppermute | solution.py:415
  150.0 0.0 collective-permute-done.other_ref
  150.0 0.7 own_part.1
  150.7 1.0 collective-permute-done.1.partner_ref
  151.6 1.4 finish.1
Async XLA Ops:
  5.2 58.0 %all-to-all-start = ((bf16[16,6,48,256]{3,2,1,0:T(8,128)(2,1)}), bf16[16,6,48,256]{3,2,1,0:T(8,128)(2,1)}, u32[]{:S(2)}, u32[]{:S(2)}) async-start(bf16[16,6,48,256]{3,2,1,0:T(8,128)(2,1)} %get-tuple-element.13), calls=%async_computation | async-start | bytes 4718592 | tf_op jit(solution)/shard_map/all_to_all | solution.py:336
  66.0 39.7 %all-to-all-start.1 = ((bf16[16,352,128]{2,1,0:T(8,128)(2,1)}), bf16[16,352,128]{2,1,0:T(8,128)(2,1)}, u32[]{:S(2)}, u32[]{:S(2)}) async-start(bf16[16,352,128]{2,1,0:T(8,128)(2,1)} %centers.1), calls=%async_computation.1 | async-start | bytes 2883584 | tf_op jit(solution)/shard_map/all_to_all | solution.py:367
  112.6 32.2 %all-to-all-start.2 = ((bf16[16,6,48,128]{3,2,1,0:T(8,128)(2,1)}), bf16[16,6,48,128]{3,2,1,0:T(8,128)(2,1)S(1)}, u32[]{:S(2)}, u32[]{:S(2)}) async-start(bf16[16,6,48,128]{3,2,1,0:T(8,128)(2,1)} %attend.1), calls=%async_computation.2 | async-start | bytes 2359296 | tf_op jit(solution)/shard_map/all_to_all | solution.py:403
  120.4 29.6 %collective-permute-start = (bf16[768,768]{1,0:T(8,128)(2,1)}, bf16[768,768]{1,0:T(8,128)(2,1)S(1)}, u32[]{:S(2)}, u32[]{:S(2)}) collective-permute-start(bf16[768,768]{1,0:T(8,128)(2,1)} %get-tuple-element.17), channel_id=1, source_target_pairs={{0,1},{1,0},{2,3},{3,2},{4,5},{5,4},{6,7},{7,6},{8,9},{9,8},{10,11... | collective-permute-start | bytes 3538952 | tf_op jit(solution)/shard_map/ppermute | solution.py:311
  144.8 0.9 copy-start
  147.4 4.2 %collective-permute-start.1 = (bf16[384,768]{1,0:T(8,128)(2,1)S(1)}, bf16[384,768]{1,0:T(8,128)(2,1)S(1)}, u32[]{:S(2)}, u32[]{:S(2)}) collective-permute-start(bf16[384,768]{1,0:T(8,128)(2,1)S(1)} %unpack.1.attended_ref), channel_id=1, source_target_pairs={{0,1},{1,0},{2,3},{3,2},{4,5},{5,4},{6,7},{7,6},{8,9},{9,8},{10,11... | collective-permute-start | bytes 1769480 | tf_op jit(solution)/shard_map/ppermute | solution.py:415
